TPU v7x, 256 devices: a whole 4x4x8 slice. The times are simulated.
256 devices in a mesh: row: 8 (over y, x_hi), pair: 32 (over z, x_lo, core).
Axes of the slice: x: 4 (x_hi: 2, x_lo: 2; x = x_hi * 2 + x_lo), y: 4, z: 8, core: 2. Of those that a mesh axis runs over, the one named last changes fastest.
Arguments:
- top_blocks: float32 [16384, 8192], P('row', 'pair'), may hold values from -60 to 60, as said below
- bottom_blocks: float32 [16384, 8192], P('row', 'pair'), may hold values from -60 to 60, as said below
Outputs:
- top_out: float32 [16384, 8192], P('row', 'pair')
- bottom_out: float32 [16384, 8192], P('row', 'pair')
Inputs may be any that keep to these rules, and one draw needn't show every extreme that they name: `top_blocks`: entries of the slab. `bottom_blocks`: entries of the slab.
All inputs are finite; a program needn't handle non-finite values.
Results may differ from a plain program's by a relative error of at most 0.00015.
Values sent between devices are 32-bit elements; how exact they have to be, the bound alone decides.
No kernel may reach another device: no remote copies, remote signals or barrier semaphores. Data moves between devices by JAX's collectives and lax.ppermute only.
A program may use at most 64 MiB of HBM per device.

v0:
```python
import functools

import jax
import jax.numpy as jnp
from jax import lax
from jax.experimental import pallas as pl
from jax.experimental.pallas import tpu as pltpu
from jax.sharding import PartitionSpec as P

STEPS = 2
SWEEPS = 3
W = 256
H = 128
PIECE = 2 * H + 8
Q = W // 4
CROSS = Q + 8
RAW = 512
MORE = 256
LAST = 768
BLOCK = 256
BF, F32 = jnp.bfloat16, jnp.float32
IN_VMEM = pl.BlockSpec(memory_space=pltpu.VMEM)
IN_SMEM = pl.BlockSpec(memory_space=pltpu.SMEM)
IN_HBM = pl.BlockSpec(memory_space=pltpu.HBM)
ANYWHERE = pl.BlockSpec(memory_space=pl.ANY)
MIB = 1024 * 1024


def granted(mib):
    return pltpu.CompilerParams(vmem_limit_bytes=mib * MIB)


def split2(x):
    high = x.astype(BF)
    return high, (x - high.astype(F32)).astype(BF)


def dot_tn(left, right):
    return lax.dot_general(left, right, (((0,), (0,)), ((), ())), preferred_element_type=F32)


def dot_nn(left, right):
    return jnp.dot(left, right, preferred_element_type=F32)


def mm3(left, right, dot=dot_nn):
    lh, ll = left
    rh, rl = right
    return dot(lh, rh) + (dot(lh, rl) + dot(ll, rh))


def mm1(left, right):
    return dot_nn(left[0], right[0])


def iotas(shape):
    return lax.broadcasted_iota(jnp.int32, shape, 0), lax.broadcasted_iota(jnp.int32, shape, 1)


def add_rows(accs, top, bottom, begin):
    th, tl = split2(top)
    bh, bl = split2(bottom)
    shares = (
        dot_tn(th, th),
        dot_tn(th, tl),
        dot_tn(bh, bh),
        dot_tn(bh, bl),
        dot_tn(th, bh) + (dot_tn(th, bl) + dot_tn(tl, bh)),
    )
    for acc, share in zip(accs, shares):
        acc[...] = share if begin else acc[...] + share


def put_pieces(accs, pieces, outs, mine):
    xtt, ytt, xbb, ybb, tb = accs
    row, col = iotas((H, H))
    upper, diag = row <= col, row == col
    for idx, (x, y) in enumerate(((xtt, ytt), (xbb, ybb))):
        full = x[...] + (y[...] + y[...].T)
        first, last = full[:H, :H], full[H:, H:]
        pieces[idx, 0:H] = full[:H, H:]
        pieces[idx, H:2 * H] = jnp.where(upper, first, last)
        line = jnp.sum(jnp.where(diag, last, 0.0), axis=0, keepdims=True)
        pieces[idx, 2 * H:PIECE] = jnp.broadcast_to(line, (8, H))
    for idx in range(2):
        half = tb[idx * H:(idx + 1) * H, :]
        pieces[2 + idx, 0:H] = half[:, :H]
        pieces[2 + idx, H:2 * H] = half[:, H:]
        pieces[2 + idx, 2 * H:PIECE] = jnp.zeros((8, H), F32)
    for ahead in range(4):
        outs[ahead][...] = pieces[(mine + ahead) % 4]


ACCS = [pltpu.VMEM((W, W), F32)] * 5
PIECES = pltpu.VMEM((4, PIECE, H), F32)


def load_kernel(top_ref, bottom_ref, out_ref, sems):
    rows = out_ref.shape[0] // 2
    copies = [
        pltpu.make_async_copy(ref.at[pl.ds(0, rows)], out_ref.at[pl.ds(side * rows, rows)], sems.at[side])
        for side, ref in enumerate((top_ref, bottom_ref))
    ]
    for copy in copies:
        copy.start()
    for copy in copies:
        copy.wait()


def loaded(top, bottom, rows):
    return pl.pallas_call(
        load_kernel,
        out_shape=jax.ShapeDtypeStruct((2 * rows, W), F32),
        in_specs=[IN_HBM, IN_HBM],
        out_specs=IN_VMEM,
        scratch_shapes=[pltpu.SemaphoreType.DMA((2,))],
        compiler_params=granted(51),
        cost_estimate=pl.CostEstimate(flops=0, bytes_accessed=16 * W * rows, transcendentals=0),
    )(top, bottom)


def first_gram_kernel(where_ref, loaded_ref, top_ref, bottom_ref, *refs):
    outs, rest, accs, pieces, sems = refs[:4], refs[4], refs[5:10], refs[10], refs[11]
    size, rows = loaded_ref.shape[0] // 2, rest.shape[0] // 2

    def copies(part):
        start = pl.multiple_of(part * size, size)
        return [
            pltpu.make_async_copy(
                ref.at[pl.ds(pl.multiple_of(start + size, size), size)],
                rest.at[pl.ds(pl.multiple_of(side * rows + start, size), size)],
                sems.at[2 * part + side],
            )
            for side, ref in enumerate((top_ref, bottom_ref))
        ]

    for part in range(rows // size):
        for copy in copies(part):
            copy.start()
    add_rows(accs, loaded_ref[:size], loaded_ref[size:], True)

    @pl.loop(0, rows // size)
    def _(part):
        for copy in copies(part):
            copy.wait()
        start = pl.multiple_of(part * size, size)
        add_rows(accs, rest[pl.ds(start, size)], rest[pl.ds(pl.multiple_of(rows + start, size), size)], False)

    put_pieces(accs, pieces, outs, where_ref[0])


def first_gram(where, own_a, top, bottom):
    rest = 2 * top.shape[0] - own_a.shape[0]
    return pl.pallas_call(
        first_gram_kernel,
        out_shape=[jax.ShapeDtypeStruct((PIECE, H), F32)] * 4 + [jax.ShapeDtypeStruct((rest, W), F32)],
        in_specs=[IN_SMEM, IN_VMEM, IN_HBM, IN_HBM],
        out_specs=[IN_VMEM] * 5,
        scratch_shapes=ACCS + [PIECES, pltpu.SemaphoreType.DMA((2 * rest // own_a.shape[0],))],
        compiler_params=granted(51),
        cost_estimate=pl.CostEstimate(flops=7 * 2 * W * W * 2048, bytes_accessed=2 ** 22, transcendentals=0),
    )(where, own_a, top, bottom)


def add_cross(cross, squares, top, bottom, begin):
    th, tl = split2(top)
    bh, bl = split2(bottom)
    share = dot_tn(th, bh) + (dot_tn(th, bl) + dot_tn(tl, bh))
    cross[...] = share if begin else cross[...] + share
    for idx, block in enumerate((top, bottom)):
        share = jnp.sum(block * block, axis=0, keepdims=True)
        squares[idx:idx + 1] = share if begin else squares[idx:idx + 1] + share


def early_cross_kernel(top_ref, bottom_ref, cross, squares):
    squares[...] = jnp.zeros_like(squares)
    add_cross(cross, squares, top_ref[:RAW], bottom_ref[:RAW], True)


def early_cross(top, bottom):
    return pl.pallas_call(
        early_cross_kernel,
        out_shape=[jax.ShapeDtypeStruct((W, W), F32), jax.ShapeDtypeStruct((8, W), F32)],
        in_specs=[IN_VMEM, IN_VMEM],
        out_specs=[IN_VMEM] * 2,
        compiler_params=granted(12),
        cost_estimate=pl.CostEstimate(flops=3 * 2 * W * W * 1024, bytes_accessed=2 ** 21, transcendentals=0),
    )(top, bottom)


def late_cross_kernel(count, where_ref, top_ref, bottom_ref, cross_ref, squares_ref, *refs):
    refs = refs[count:]
    outs, ship, cross, squares, pieces, sems = refs[:4], refs[4], refs[5], refs[6], refs[7], refs[8]
    late = top_ref.shape[0]
    early, mid = bottom_ref.shape[0] - late, (ship.shape[0] + MORE) // 2
    copies = [
        pltpu.make_async_copy(top_ref.at[pl.ds(0, mid)], ship.at[pl.ds(0, mid)], sems.at[0]),
        pltpu.make_async_copy(
            bottom_ref.at[pl.ds(early + MORE, mid - MORE)], ship.at[pl.ds(mid, mid - MORE)], sems.at[1]
        ),
    ]
    for copy in copies:
        copy.start()
    cross[...] = cross_ref[...]
    squares[...] = squares_ref[...]

    @pl.loop(0, top_ref.shape[0] // 512)
    def _(step):
        begin = pl.multiple_of(step * 512, 512)
        add_cross(cross, squares, top_ref[pl.ds(begin, 512)], bottom_ref[pl.ds(early + begin, 512)], False)

    for idx in range(4):
        pieces[idx, :Q] = cross[idx * Q:(idx + 1) * Q]
        pieces[idx, Q:] = squares[...] if idx == 0 else jnp.zeros_like(squares)
    for ahead in range(4):
        outs[ahead][...] = pieces[(where_ref[0] + ahead) % 4]
    for copy in copies:
        copy.wait()


def late_cross(where, top, bottom, before, mid, after):
    return pl.pallas_call(
        functools.partial(late_cross_kernel, len(after)),
        out_shape=[jax.ShapeDtypeStruct((CROSS, W), F32)] * 4 + [jax.ShapeDtypeStruct((2 * mid - MORE, W), F32)],
        in_specs=[IN_SMEM] + [IN_VMEM] * 4 + [ANYWHERE] * len(after),
        out_specs=[IN_VMEM] * 5,
        scratch_shapes=[
            pltpu.VMEM((W, W), F32), pltpu.VMEM((8, W), F32), pltpu.VMEM((4, CROSS, W), F32),
            pltpu.SemaphoreType.DMA((2,)),
        ],
        compiler_params=granted(12),
        cost_estimate=pl.CostEstimate(flops=3 * 2 * W * W * 1024, bytes_accessed=2 ** 21, transcendentals=0),
    )(where, top, bottom, *before, *after)


def turned_gram_kernel(count, gram_ref, *refs):
    whole = split2(gram_ref[...])
    for ref, out in zip(refs[:count], refs[count:]):
        turn = split2(ref[...])
        out[...] = mm3(turn, split2(mm3(whole, turn)), dot_tn)


def turned_grams(gram, *turns):
    return pl.pallas_call(
        functools.partial(turned_gram_kernel, len(turns)),
        out_shape=[jax.ShapeDtypeStruct((W, W), F32)] * len(turns),
        in_specs=[IN_VMEM] * (1 + len(turns)),
        out_specs=[IN_VMEM] * len(turns),
        compiler_params=granted(16),
        cost_estimate=pl.CostEstimate(flops=3 * (2 * W) ** 3 * len(turns), bytes_accessed=2 ** 21, transcendentals=0),
    )(gram, *turns)


def turn_columns(gram, sq_line, sq_col):
    sq_line, sq_col = sq_line + 1e-06, sq_col + 1e-06
    corr = gram * (1.0 / jnp.sqrt(sq_col)) * (1.0 / jnp.sqrt(sq_line))
    generator = corr * ((sq_line - sq_col) / (sq_line + sq_col))
    frobenius = jnp.sqrt(jnp.sum(generator * generator))
    skew = generator * (1.0 / (1.0 + frobenius))

    s2 = split2(skew)
    n = -mm3(s2, s2)
    n_2 = split2(n)
    nn = mm3(n_2, n_2)
    d1 = 0.25 * mm1(split2(nn), n_2) - 0.75 * nn
    d1_2 = split2(d1)
    dd = mm1(d1_2, d1_2)
    d2 = 0.25 * mm1(split2(dd), d1_2) - 0.75 * dd
    x = 0.5 * (d1 + d2) - 0.25 * mm1(d1_2, split2(d2))
    y = 0.5 * n + x - 0.5 * mm1(n_2, split2(x))
    row, col = iotas((2 * W, 2 * W))
    return jnp.where(row == col, 1.0, skew) - (y + mm3(s2, split2(y)))


def rotation_kernel(where_ref, q0, q1, q2, q3, *refs):
    first_ref, second_ref, gram, pieces = refs[-4:]
    mine = where_ref[0]
    for behind, piece in enumerate((q0, q1, q2, q3)):
        pieces[(mine + 4 - behind) % 4] = piece[...]
    row, col = iotas((H, H))
    upper, diag = row <= col, row == col

    def put(i, j, block):
        gram[i * H:(i + 1) * H, j * H:(j + 1) * H] = block

    lines, columns = [], []
    for half in range(2):
        off = pieces[half, 0:H]
        both = pieces[half, H:2 * H]
        line = pieces[half, 2 * H:2 * H + 1]
        turned = both.T
        first = jnp.where(upper, both, turned)
        last = jnp.where(diag, line, jnp.where(upper, turned, both))
        a, b = 2 * half, 2 * half + 1
        put(a, b, off)
        put(b, a, off.T)
        put(a, a, first)
        put(b, b, last)
        for block in (first, last):
            on = jnp.where(diag, block, 0.0)
            lines.append(jnp.sum(on, axis=0, keepdims=True))
            columns.append(jnp.sum(on, axis=1, keepdims=True))
    for i in range(2):
        for j in range(2):
            block = pieces[2 + i, j * H:(j + 1) * H]
            put(i, 2 + j, block)
            put(2 + j, i, block.T)
    rotate = turn_columns(gram[...], jnp.concatenate(lines, axis=1), jnp.concatenate(columns, axis=0))
    first_ref[...] = rotate[:, :W]
    second_ref[...] = rotate[:, W:]


def rotation(where, quarters, after=()):
    half = jax.ShapeDtypeStruct((2 * W, W), F32)
    return pl.pallas_call(
        rotation_kernel,
        out_shape=[half, half, jax.ShapeDtypeStruct((2 * W, 2 * W), F32)],
        in_specs=[IN_SMEM] + [IN_VMEM] * 4 + [ANYWHERE] * len(after),
        out_specs=[IN_VMEM] * 3,
        scratch_shapes=[PIECES],
        compiler_params=granted(20),
        cost_estimate=pl.CostEstimate(flops=14 * 2 * (2 * W) ** 3, bytes_accessed=2 ** 21, transcendentals=0),
    )(where, *quarters, *after)


def second_rotation_kernel(where_ref, q0, q1, q2, q3, top_ref, bottom_ref, first_ref, second_ref, pieces, gram):
    mine = where_ref[0]
    for behind, piece in enumerate((q0, q1, q2, q3)):
        pieces[(mine + 4 - behind) % 4] = piece[...]
    for idx in range(4):
        rows = slice(idx * Q, (idx + 1) * Q)
        gram[rows, W:] = pieces[idx, :Q]
    gram[:W, :W] = top_ref[...]
    gram[W:, W:] = bottom_ref[...]
    gram[W:, :W] = gram[:W, W:].T
    row, col = iotas((W, W))
    lines, columns = [], []
    for idx in range(2):
        line = pieces[0, Q + idx:Q + idx + 1]
        lines.append(line)
        columns.append(jnp.sum(jnp.where(row == col, line, 0.0), axis=1, keepdims=True))
    rotate = turn_columns(gram[...], jnp.concatenate(lines, axis=1), jnp.concatenate(columns, axis=0))
    first_ref[...] = rotate[:, :W]
    second_ref[...] = rotate[:, W:]


def second_rotation(where, quarters, top_gram, bottom_gram):
    half = jax.ShapeDtypeStruct((2 * W, W), F32)
    return pl.pallas_call(
        second_rotation_kernel,
        out_shape=[half, half],
        in_specs=[IN_SMEM] + [IN_VMEM] * 6,
        out_specs=[IN_VMEM] * 2,
        scratch_shapes=[pltpu.VMEM((4, CROSS, W), F32), pltpu.VMEM((2 * W, 2 * W), F32)],
        compiler_params=granted(20),
        cost_estimate=pl.CostEstimate(flops=14 * 2 * (2 * W) ** 3, bytes_accessed=2 ** 21, transcendentals=0),
    )(where, *quarters, top_gram, bottom_gram)


def apply_kernel(jobs, moves, n_in, n_turn, n_after, to_hbm, rolled, *refs):
    refs = refs[:n_in + n_turn] + refs[n_in + n_turn + n_after:]
    blocks, turns = refs[:n_in], [split2(ref[:2 * W]) for ref in refs[n_in:n_in + n_turn]]
    outs, scratch = refs[n_in + n_turn:n_in + n_turn + len(to_hbm)], refs[n_in + n_turn + len(to_hbm):]
    held, copies = list(outs), []
    for idx, hbm in enumerate(to_hbm):
        if hbm:
            held[idx] = scratch[2 * sum(to_hbm[:idx])]
    for top, top_start, bottom, bottom_start, rows, turn, places in jobs:
        high, low = turns[turn]

        def work(begin, size, top=top, top_start=top_start, bottom=bottom, bottom_start=bottom_start):
            first = split2(blocks[top][pl.ds(top_start + begin, size)])
            second = split2(blocks[bottom][pl.ds(bottom_start + begin, size)])
            return mm3(first, (high[:W], low[:W])) + mm3(second, (high[W:], low[W:]))

        if places[0][0] >= rolled[1]:
            @pl.loop(0, rows // rolled[0])
            def _(step):
                begin = pl.multiple_of(step * rolled[0], rolled[0])
                block = work(begin, rolled[0])
                for out, start in places:
                    held[out][pl.ds(start + begin, rolled[0])] = block
        else:
            for begin in range(0, rows, BLOCK):
                block = work(begin, BLOCK)
                for out, start in places:
                    held[out][start + begin:start + begin + BLOCK] = block
        for out, start in places:
            if to_hbm[out]:
                span, sems = pl.ds(start, rows), scratch[2 * sum(to_hbm[:out]) + 1]
                copies.append(pltpu.make_async_copy(held[out].at[span], outs[out].at[span], sems.at[len(copies)]))
                copies[-1].start()
    for source, start, rows, out, out_start in moves:
        held[out][out_start:out_start + rows] = refs[source][start:start + rows]
    for copy in copies:
        copy.wait()


def rotated(jobs, outs, moves=(), after=(), rolled=(BLOCK, 9)):
    arrays, turns = [], []

    def index(array, known):
        for idx, other in enumerate(known):
            if other is array:
                return idx
        known.append(array)
        return len(known) - 1

    listed, count = [], 0
    for top, top_start, bottom, bottom_start, rows, turn, places in jobs:
        count += rows
        listed.append((index(top, arrays), top_start, index(bottom, arrays), bottom_start, rows, index(turn, turns),
                       tuple(places)))
    copied = [(index(array, arrays), start, rows, out, row) for array, start, rows, out, row in moves]
    scratch = []
    for rows, hbm in outs:
        if hbm:
            scratch += [pltpu.VMEM((rows, W), F32), pltpu.SemaphoreType.DMA((8,))]
    result = pl.pallas_call(
        functools.partial(apply_kernel, listed, copied, len(arrays), len(turns), len(after), [hbm for _, hbm in outs], rolled),
        out_shape=[jax.ShapeDtypeStruct((rows, W), F32) for rows, _ in outs],
        in_specs=[IN_VMEM] * (len(arrays) + len(turns)) + [ANYWHERE] * len(after),
        out_specs=[IN_HBM if hbm else IN_VMEM for _, hbm in outs],
        scratch_shapes=scratch,
        compiler_params=granted(12),
        cost_estimate=pl.CostEstimate(flops=6 * 2 * W * W * count, bytes_accessed=12 * W * count, transcendentals=0),
    )(*arrays, *turns, *after)
    return result


def sum_kernel(count, *refs):
    refs[-1][...] = functools.reduce(lambda a, b: a + b, [ref[...] for ref in refs[:count]])


def summed(terms, after):
    return pl.pallas_call(
        functools.partial(sum_kernel, len(terms)),
        out_shape=jax.ShapeDtypeStruct(terms[0].shape, F32),
        in_specs=[IN_VMEM] * len(terms) + [ANYWHERE] * len(after),
        out_specs=IN_VMEM,
        compiler_params=granted(2),
    )(*terms, *after)


def tie_kernel(*refs):
    pass


def tied(array, after):
    return pl.pallas_call(
        tie_kernel,
        out_shape=jax.ShapeDtypeStruct(array.shape, F32),
        in_specs=[ANYWHERE] * (1 + len(after)),
        out_specs=ANYWHERE,
        input_output_aliases={0: 0},
        compiler_params=granted(1),
    )(array, *after)


def last_kernel(count, *refs):
    parts, out_ref, sems = refs[:count], refs[count + 1], refs[count + 2]
    at, copies = out_ref.shape[0], []
    for idx in reversed(range(count)):
        rows = parts[idx].shape[0]
        at -= rows
        copies.append(pltpu.make_async_copy(parts[idx], out_ref.at[pl.ds(at, rows)], sems.at[idx]))
        copies[-1].start()
    for copy in copies:
        copy.wait()


def with_last(whole, parts):
    return pl.pallas_call(
        functools.partial(last_kernel, len(parts)),
        out_shape=jax.ShapeDtypeStruct(whole.shape, F32),
        in_specs=[IN_VMEM] * len(parts) + [IN_HBM],
        out_specs=IN_HBM,
        scratch_shapes=[pltpu.SemaphoreType.DMA((len(parts),))],
        input_output_aliases={len(parts): 0},
        compiler_params=granted(2),
    )(*parts, whole)


def passed_along(array, by=1):
    length = lax.axis_size("pair")
    return lax.ppermute(array, "pair", [(i, (i + by) % length) for i in range(length)])


def along_y(array, by):
    length = lax.axis_size("row") // 2
    return lax.ppermute(
        array, "row", [(2 * y + h, 2 * ((y + by) % length) + h) for y in range(length) for h in range(2)]
    )


def across_x(array):
    return lax.ppermute(array, "row", [(i, i ^ 1) for i in range(lax.axis_size("row"))])


def scattered(pieces, after):
    return summed([pieces[0]] + [along_y(pieces[r], r) for r in (1, 2, 3)], after)


def gathered_quarters(total):
    return [total] + [along_y(total, r) for r in (1, 2, 3)]


def on_device(top, bottom):
    where = (lax.axis_index("row") // 2).astype(jnp.int32).reshape(1)
    rows = top.shape[0]
    late = rows - RAW
    mid = late - LAST

    own_a = loaded(top, bottom, RAW)
    raw = passed_along(own_a)
    *pieces, own_b = first_gram(where, own_a, top, bottom)
    total = scattered(pieces, [])
    total = summed([total, across_x(total)], [raw])
    total_prev = passed_along(total)
    first, second, whole = rotation(where, gathered_quarters(total))
    (sent,) = rotated([(own_b, 0, own_b, late, late, first, [(0, 0)])], [(late, False)], after=[total_prev], rolled=(BLOCK, 0))
    quarters_prev = gathered_quarters(tied(total_prev, [sent]))
    sent = passed_along(sent)
    (bottom,) = rotated(
        [(own_a, 0, own_a, RAW, RAW, second, [(0, 0)]), (own_b, 0, own_b, late, late, second, [(0, RAW)])],
        [(rows, False)],
        rolled=(BLOCK, 0),
    )
    (bottom_gram,) = turned_grams(whole, second)
    first_prev, second_prev, whole_prev = rotation(where, quarters_prev, [bottom_gram])
    (early,) = rotated(
        [(raw, 0, raw, RAW, RAW, first_prev, [(0, 0)])], [(RAW + MORE, False)], [(bottom, RAW, MORE, 0, RAW)],
        rolled=(BLOCK, 0),
    )
    early_prev = passed_along(early)
    (top_gram,) = turned_grams(whole_prev, first_prev)

    *pieces, ship = late_cross(
        where, sent, bottom, early_cross(early, bottom), mid, []
    )
    total = scattered(pieces, [early_prev, top_gram])
    total = total + across_x(total)
    ship = passed_along(tied(ship, [total]))
    (bottom_prev,) = rotated(
        [(raw, 0, raw, RAW, RAW, second_prev, [(0, 0)])], [(RAW, False)], rolled=(BLOCK, 0)
    )
    first, second = second_rotation(where, gathered_quarters(total), top_gram, bottom_gram)
    first_prev = passed_along(first)
    *out_late, bottom_out = rotated(
        [
            (sent, mid, bottom, RAW + mid, LAST - W, first, [(0, 0)]),
            (sent, late - W, bottom, rows - W, W, first, [(1, 0)]),
            (early, 0, bottom, 0, RAW, second, [(2, 0)]),
            (sent, 0, bottom, RAW, late, second, [(2, RAW)]),
        ],
        [(LAST - W, False), (W, False), (rows, True)],
        rolled=(BLOCK, 2),
    )
    out_late = [passed_along(part) for part in out_late]
    (top_out,) = rotated(
        [
            (early_prev, 0, bottom_prev, 0, RAW, first_prev, [(0, 0)]),
            (ship, 0, early_prev, RAW, MORE, first_prev, [(0, RAW)]),
            (ship, MORE, ship, mid, mid - MORE, first_prev, [(0, RAW + MORE)]),
        ],
        [(rows, True)],
        rolled=(BLOCK, 0),
    )
    return (with_last(top_out, out_late), bottom_out)


def solution(mesh):
    placed = (P("row", "pair"), P("row", "pair"))
    return jax.shard_map(on_device, mesh=mesh, in_specs=placed, out_specs=placed, check_vma=False)
```

profile of v0, /device:TPU:128, one launch (start us, length us, event | category | flops | bytes accessed | tf_op | source)
XLA Modules:
  0.0 117.0 jit_solution(15977996709304598338)
XLA Ops:
  2.0 4.3 %shard_map.42 = (f32[264,128]{1,0:T(8,128)S(1)}, f32[264,128]{1,0:T(8,128)S(1)}, f32[264,128]{1,0:T(8,128)S(1)}, f32[264,128]{1,0:T(8,128)S(1)}, f32[3072,256]{1,0:T(8,128)}) custom-call(s32[1]{0:T(128)} %bitcast.where_ref, f32[1024,256]{1,0:T(8,128)S(1)} %shard_map.41.loaded_ref.refs_0_, f32[2048,256]{1,0:T(8,128)} %top_ref.3, f32[2048,256]{1,0:T(8,128)} %bottom_ref.3), custom_call_target="tpu_custom_call" | custom-call | flops 1879048192 | bytes 4194304 | tf_op jit(solution)/shard_map/pallas_call | solution.py:154
  8.0 2.9 %collective-permute-start.1 = (f32[264,128]{1,0:T(8,128)S(1)}, f32[264,128]{1,0:T(8,128)S(1)}, u32[]{:S(2)}, u32[]{:S(2)}) collective-permute-start(f32[264,128]{1,0:T(8,128)S(1)} %get-tuple-element.28), channel_id=1, source_target_pairs={{0,128},{32,160},{64,192},{96,224},{128,0},{160,32},{192,64},{224,... | collective-permute-start | bytes 405512 | tf_op jit(solution)/shard_map/ppermute | solution.py:491
  13.4 4.2 %collective-permute-done.1.refs_2_ = f32[264,128]{1,0:T(8,128)S(1)} collective-permute-done((f32[264,128]{1,0:T(8,128)S(1)}, f32[264,128]{1,0:T(8,128)S(1)}, u32[]{:S(2)}, u32[]{:S(2)}) %collective-permute-start.1) | collective-permute-done | bytes 135200 | tf_op jit(solution)/shard_map/ppermute | solution.py:491
  17.7 3.3 %collective-permute-start.3 = (f32[264,128]{1,0:T(8,128)S(1)}, f32[264,128]{1,0:T(8,128)S(1)}, u32[]{:S(2)}, u32[]{:S(2)}) collective-permute-start(f32[264,128]{1,0:T(8,128)S(1)} %shard_map.43.refs_0_), channel_id=1, source_target_pairs={{0,32},{32,0},{64,96},{96,64},{128,160},{160,128},{192,224},{224,1... | collective-permute-start | bytes 405512 | tf_op jit(solution)/shard_map/ppermute | solution.py:497
  21.0 4.4 %collective-permute-done.3.refs_1_ = f32[264,128]{1,0:T(8,128)S(1)} collective-permute-done((f32[264,128]{1,0:T(8,128)S(1)}, f32[264,128]{1,0:T(8,128)S(1)}, u32[]{:S(2)}, u32[]{:S(2)}) %collective-permute-start.3) | collective-permute-done | bytes 135200 | tf_op jit(solution)/shard_map/ppermute | solution.py:497
  25.5 2.4 %collective-permute-start.7 = (f32[264,128]{1,0:T(8,128)S(1)}, f32[264,128]{1,0:T(8,128)S(1)}, u32[]{:S(2)}, u32[]{:S(2)}) collective-permute-start(f32[264,128]{1,0:T(8,128)S(1)} %shard_map.44.q0), channel_id=1, source_target_pairs={{0,192},{32,224},{64,0},{96,32},{128,64},{160,96},{192,128},{224,1... | collective-permute-start | bytes 405512 | tf_op jit(solution)/shard_map/ppermute | solution.py:491
  29.8 3.4 %collective-permute-done.7.q3 = f32[264,128]{1,0:T(8,128)S(1)} collective-permute-done((f32[264,128]{1,0:T(8,128)S(1)}, f32[264,128]{1,0:T(8,128)S(1)}, u32[]{:S(2)}, u32[]{:S(2)}) %collective-permute-start.7) | collective-permute-done | bytes 135200 | tf_op jit(solution)/shard_map/ppermute | solution.py:491
  36.7 5.4 %shard_map.45 = (f32[512,256]{1,0:T(8,128)S(1)}, f32[512,256]{1,0:T(8,128)S(1)}, f32[512,512]{1,0:T(8,128)S(1)}) custom-call(s32[1]{0:T(128)} %bitcast.where_ref, f32[264,128]{1,0:T(8,128)S(1)} %shard_map.44.q0, f32[264,128]{1,0:T(8,128)S(1)} %collective-permute-done.5.q1, f32[264,128]{1,0:T(8,128)S(1)} %collective-permute-done.6.q2, ...), custom_call_target="tpu_custom_call" | custom-call | flops 3758096384 | bytes 2097152 | tf_op jit(solution)/shard_map/pallas_call | solution.py:315
  42.2 2.4 %shard_map.46.refs_1_ = f32[1536,256]{1,0:T(8,128)S(1)} custom-call(f32[3072,256]{1,0:T(8,128)S(1)} %copy-done, f32[512,256]{1,0:T(8,128)S(1)} %get-tuple-element.30.refs_1_, f32[264,128]{1,0:T(8,128)S(1)} %collective-permute-done.8.refs_2_.refs_0_), custom_call_target="tpu_custom_call" | custom-call | flops 1207959552 | bytes 4718592 | tf_op jit(solution)/shard_map/pallas_call | solution.py:419
  49.3 3.1 %shard_map.47.refs_1_.bottom_ref = f32[2048,256]{1,0:T(8,128)S(1)} custom-call(f32[1024,256]{1,0:T(8,128)S(1)} %shard_map.41.loaded_ref.refs_0_, f32[3072,256]{1,0:T(8,128)S(1)} %copy-done, f32[512,256]{1,0:T(8,128)S(1)} %get-tuple-element.31.refs_2_.refs_0_), custom_call_target="tpu_custom_call" | custom-call | flops 1610612736 | bytes 6291456 | tf_op jit(solution)/shard_map/pallas_call | solution.py:419
  53.4 3.0 %collective-permute-done.10.q1 = f32[264,128]{1,0:T(8,128)S(1)} collective-permute-done((f32[264,128]{1,0:T(8,128)S(1)}, f32[264,128]{1,0:T(8,128)S(1)}, u32[]{:S(2)}, u32[]{:S(2)}) %collective-permute-start.10) | collective-permute-done | bytes 135200 | tf_op jit(solution)/shard_map/ppermute | solution.py:491
  56.4 5.4 %shard_map.50 = (f32[512,256]{1,0:T(8,128)S(1)}, f32[512,256]{1,0:T(8,128)S(1)}, f32[512,512]{1,0:T(8,128)S(1)}) custom-call(s32[1]{0:T(128)} %bitcast.where_ref, f32[264,128]{1,0:T(8,128)S(1)} %shard_map.48.q0, f32[264,128]{1,0:T(8,128)S(1)} %collective-permute-done.10.q1, f32[264,128]{1,0:T(8,128)S(1)} %collective-permute-done.11.q2, ...), custom_call_target="tpu_custom_call" | custom-call | flops 3758096384 | bytes 2097152 | tf_op jit(solution)/shard_map/pallas_call | solution.py:315
  63.2 3.6 %collective-permute-done.9.top_ref.refs_0_ = f32[1536,256]{1,0:T(8,128)S(1)} collective-permute-done((f32[1536,256]{1,0:T(8,128)S(1)}, f32[1536,256]{1,0:T(8,128)S(1)}, u32[]{:S(2)}, u32[]{:S(2)}) %collective-permute-start.9) | collective-permute-done | bytes 1572896 | tf_op jit(solution)/shard_map/ppermute | solution.py:486
  70.5 2.2 %collective-permute-start.15 = (f32[72,256]{1,0:T(8,128)S(1)}, f32[72,256]{1,0:T(8,128)S(1)}, u32[]{:S(2)}, u32[]{:S(2)}) collective-permute-start(f32[72,256]{1,0:T(8,128)S(1)} %get-tuple-element.39), channel_id=1, source_target_pairs={{0,192},{32,224},{64,0},{96,32},{128,64},{160,96},{192,128},{224,1... | collective-permute-start | bytes 221192 | tf_op jit(solution)/shard_map/ppermute | solution.py:491
  74.0 2.3 %collective-permute-done.16.refs_4_.refs_0_ = f32[768,256]{1,0:T(8,128)S(1)} collective-permute-done((f32[768,256]{1,0:T(8,128)S(1)}, f32[768,256]{1,0:T(8,128)S(1)}, u32[]{:S(2)}, u32[]{:S(2)}) %collective-permute-start.16) | collective-permute-done | bytes 786464 | tf_op jit(solution)/shard_map/ppermute | solution.py:486
  76.3 3.3 %collective-permute-start.17 = (f32[72,256]{1,0:T(8,128)S(1)}, f32[72,256]{1,0:T(8,128)S(1)}, u32[]{:S(2)}, u32[]{:S(2)}) collective-permute-start(f32[72,256]{1,0:T(8,128)S(1)} %shard_map.55), channel_id=1, source_target_pairs={{0,32},{32,0},{64,96},{96,64},{128,160},{160,128},{192,224},{224,1... | collective-permute-start | bytes 221192 | tf_op jit(solution)/shard_map/ppermute | solution.py:497
  79.5 2.9 %collective-permute-done.17 = f32[72,256]{1,0:T(8,128)S(1)} collective-permute-done((f32[72,256]{1,0:T(8,128)S(1)}, f32[72,256]{1,0:T(8,128)S(1)}, u32[]{:S(2)}, u32[]{:S(2)}) %collective-permute-start.17) | collective-permute-done | bytes 73760 | tf_op jit(solution)/shard_map/ppermute | solution.py:497
  82.6 2.2 %collective-permute-start.20 = (f32[72,256]{1,0:T(8,128)S(1)}, f32[72,256]{1,0:T(8,128)S(1)}, u32[]{:S(2)}, u32[]{:S(2)}) collective-permute-start(f32[72,256]{1,0:T(8,128)S(1)} %add.4.q0.refs_1_), channel_id=1, source_target_pairs={{0,192},{32,224},{64,0},{96,32},{128,64},{160,96},{192,128},{224,1... | collective-permute-start | bytes 221192 | tf_op jit(solution)/shard_map/ppermute | solution.py:491
  87.5 3.2 %collective-permute-done.19.q2 = f32[72,256]{1,0:T(8,128)S(1)} collective-permute-done((f32[72,256]{1,0:T(8,128)S(1)}, f32[72,256]{1,0:T(8,128)S(1)}, u32[]{:S(2)}, u32[]{:S(2)}) %collective-permute-start.19) | collective-permute-done | bytes 73760 | tf_op jit(solution)/shard_map/ppermute | solution.py:491
  91.4 5.3 %shard_map.56 = (f32[512,256]{1,0:T(8,128)S(1)}, f32[512,256]{1,0:T(8,128)S(1)}) custom-call(s32[1]{0:T(128)} %bitcast.where_ref, f32[72,256]{1,0:T(8,128)S(1)} %add.4.q0.refs_1_, f32[72,256]{1,0:T(8,128)S(1)} %collective-permute-done.18.q1, f32[72,256]{1,0:T(8,128)S(1)} %collective-permute-done.19.q2, f32[72,256]{1,0:T(8,128)S(1)} %collective-permute-done.20.q3, ...), custom_call_target="tpu_custom_call" | custom-call | flops 3758096384 | bytes 2097152 | tf_op jit(solution)/shard_map/pallas_call | solution.py:349
  96.8 5.4 %shard_map.57 = (f32[512,256]{1,0:T(8,128)S(1)}, f32[256,256]{1,0:T(8,128)S(1)}, f32[2048,256]{1,0:T(8,128)}) custom-call(f32[1536,256]{1,0:T(8,128)S(1)} %collective-permute-done.9.top_ref.refs_0_, f32[2048,256]{1,0:T(8,128)S(1)} %shard_map.47.refs_1_.bottom_ref, f32[768,256]{1,0:T(8,128)S(1)} %shard_map.51.top_ref.refs_2_, ...), custom_call_target="tpu_custom_call" | custom-call | flops 2214592512 | bytes 8650752 | tf_op jit(solution)/shard_map/pallas_call | solution.py:419
  103.7 3.8 %collective-permute-done.24.refs_3_ = f32[512,256]{1,0:T(8,128)S(1)} collective-permute-done((f32[512,256]{1,0:T(8,128)S(1)}, f32[512,256]{1,0:T(8,128)S(1)}, u32[]{:S(2)}, u32[]{:S(2)}) %collective-permute-start.24) | collective-permute-done | bytes 524320 | tf_op jit(solution)/shard_map/ppermute | solution.py:486
  107.5 2.9 %shard_map.60.refs_2_ = f32[2048,256]{1,0:T(8,128)} custom-call(f32[768,256]{1,0:T(8,128)S(1)} %collective-permute-done.16.refs_4_.refs_0_, f32[512,256]{1,0:T(8,128)S(1)} %shard_map.58.refs_1_, f32[1280,256]{1,0:T(8,128)S(1)} %collective-permute-done.23.refs_2_, f32[512,256]{1,0:T(8,128)S(1)} %collective-permute-done.24.refs_3_), custom_call_target="tpu_custom_call" | custom-call | flops 1006632960 | bytes 3932160 | tf_op jit(solution)/shard_map/pallas_call | solution.py:419
  110.4 5.6 %collective-permute-done.22.refs_1_ = f32[256,256]{1,0:T(8,128)S(1)} collective-permute-done((f32[256,256]{1,0:T(8,128)S(1)}, f32[256,256]{1,0:T(8,128)S(1)}, u32[]{:S(2)}, u32[]{:S(2)}) %collective-permute-start.22) | collective-permute-done | bytes 262176 | tf_op jit(solution)/shard_map/ppermute | solution.py:486
  (50 shorter events, 29.3 us)
Async XLA Ops:
  1.9 23.6 %collective-permute-start.4 = (f32[1024,256]{1,0:T(8,128)S(1)}, f32[1024,256]{1,0:T(8,128)S(1)}, u32[]{:S(2)}, u32[]{:S(2)}) collective-permute-start(f32[1024,256]{1,0:T(8,128)S(1)} %shard_map.41.loaded_ref.refs_0_), channel_id=1, source_target_pairs={{0,1},{1,2},{2,3},{3,4},{4,5},{5,6},{6,7},{7,8},{8,9},{9,10},{10,1... | collective-permute-start | bytes 3145736 | tf_op jit(solution)/shard_map/ppermute | solution.py:486
  6.3 7.1 %collective-permute-start = (f32[264,128]{1,0:T(8,128)S(1)}, f32[264,128]{1,0:T(8,128)S(1)}, u32[]{:S(2)}, u32[]{:S(2)}) collective-permute-start(f32[264,128]{1,0:T(8,128)S(1)} %get-tuple-element.27), channel_id=1, source_target_pairs={{0,64},{32,96},{64,128},{96,160},{128,192},{160,224},{192,0},{224,... | collective-permute-start | bytes 405512 | tf_op jit(solution)/shard_map/ppermute | solution.py:491
  8.0 9.7 %collective-permute-start.1 = (f32[264,128]{1,0:T(8,128)S(1)}, f32[264,128]{1,0:T(8,128)S(1)}, u32[]{:S(2)}, u32[]{:S(2)}) collective-permute-start(f32[264,128]{1,0:T(8,128)S(1)} %get-tuple-element.28), channel_id=1, source_target_pairs={{0,128},{32,160},{64,192},{96,224},{128,0},{160,32},{192,64},{224,... | collective-permute-start | bytes 405512 | tf_op jit(solution)/shard_map/ppermute | solution.py:491
  10.9 6.8 %collective-permute-start.2 = (f32[264,128]{1,0:T(8,128)S(1)}, f32[264,128]{1,0:T(8,128)S(1)}, u32[]{:S(2)}, u32[]{:S(2)}) collective-permute-start(f32[264,128]{1,0:T(8,128)S(1)} %get-tuple-element.29), channel_id=1, source_target_pairs={{0,192},{32,224},{64,0},{96,32},{128,64},{160,96},{192,128},{224,1... | collective-permute-start | bytes 405512 | tf_op jit(solution)/shard_map/ppermute | solution.py:491
  17.7 7.7 %collective-permute-start.3 = (f32[264,128]{1,0:T(8,128)S(1)}, f32[264,128]{1,0:T(8,128)S(1)}, u32[]{:S(2)}, u32[]{:S(2)}) collective-permute-start(f32[264,128]{1,0:T(8,128)S(1)} %shard_map.43.refs_0_), channel_id=1, source_target_pairs={{0,32},{32,0},{64,96},{96,64},{128,160},{160,128},{192,224},{224,1... | collective-permute-start | bytes 405512 | tf_op jit(solution)/shard_map/ppermute | solution.py:497
  25.5 7.7 %collective-permute-start.7 = (f32[264,128]{1,0:T(8,128)S(1)}, f32[264,128]{1,0:T(8,128)S(1)}, u32[]{:S(2)}, u32[]{:S(2)}) collective-permute-start(f32[264,128]{1,0:T(8,128)S(1)} %shard_map.44.q0), channel_id=1, source_target_pairs={{0,192},{32,224},{64,0},{96,32},{128,64},{160,96},{192,128},{224,1... | collective-permute-start | bytes 405512 | tf_op jit(solution)/shard_map/ppermute | solution.py:491
  27.8 7.5 %collective-permute-start.6 = (f32[264,128]{1,0:T(8,128)S(1)}, f32[264,128]{1,0:T(8,128)S(1)}, u32[]{:S(2)}, u32[]{:S(2)}) collective-permute-start(f32[264,128]{1,0:T(8,128)S(1)} %shard_map.44.q0), channel_id=1, source_target_pairs={{0,128},{32,160},{64,192},{96,224},{128,0},{160,32},{192,64},{224,... | collective-permute-start | bytes 405512 | tf_op jit(solution)/shard_map/ppermute | solution.py:491
  29.3 7.5 %collective-permute-start.5 = (f32[264,128]{1,0:T(8,128)S(1)}, f32[264,128]{1,0:T(8,128)S(1)}, u32[]{:S(2)}, u32[]{:S(2)}) collective-permute-start(f32[264,128]{1,0:T(8,128)S(1)} %shard_map.44.q0), channel_id=1, source_target_pairs={{0,64},{32,96},{64,128},{96,160},{128,192},{160,224},{192,0},{224,... | collective-permute-start | bytes 405512 | tf_op jit(solution)/shard_map/ppermute | solution.py:491
  29.8 12.3 %collective-permute-start.8 = (f32[264,128]{1,0:T(8,128)S(1)}, f32[264,128]{1,0:T(8,128)S(1)}, u32[]{:S(2)}, u32[]{:S(2)}) collective-permute-start(f32[264,128]{1,0:T(8,128)S(1)} %shard_map.44.q0), channel_id=1, source_target_pairs={{0,1},{1,2},{2,3},{3,4},{4,5},{5,6},{6,7},{7,8},{8,9},{9,10},{10,1... | collective-permute-start | bytes 405512 | tf_op jit(solution)/shard_map/ppermute | solution.py:486
  44.6 22.2 %collective-permute-start.9 = (f32[1536,256]{1,0:T(8,128)S(1)}, f32[1536,256]{1,0:T(8,128)S(1)}, u32[]{:S(2)}, u32[]{:S(2)}) collective-permute-start(f32[1536,256]{1,0:T(8,128)S(1)} %shard_map.46.refs_1_), channel_id=1, source_target_pairs={{0,1},{1,2},{2,3},{3,4},{4,5},{5,6},{6,7},{7,8},{8,9},{9,10},{10,1... | collective-permute-start | bytes 4718600 | tf_op jit(solution)/shard_map/ppermute | solution.py:486
  44.9 7.5 %collective-permute-start.12 = (f32[264,128]{1,0:T(8,128)S(1)}, f32[264,128]{1,0:T(8,128)S(1)}, u32[]{:S(2)}, u32[]{:S(2)}) collective-permute-start(f32[264,128]{1,0:T(8,128)S(1)} %shard_map.48.q0), channel_id=1, source_target_pairs={{0,192},{32,224},{64,0},{96,32},{128,64},{160,96},{192,128},{224,1... | collective-permute-start | bytes 405512 | tf_op jit(solution)/shard_map/ppermute | solution.py:491
  45.5 7.9 %collective-permute-start.11 = (f32[264,128]{1,0:T(8,128)S(1)}, f32[264,128]{1,0:T(8,128)S(1)}, u32[]{:S(2)}, u32[]{:S(2)}) collective-permute-start(f32[264,128]{1,0:T(8,128)S(1)} %shard_map.48.q0), channel_id=1, source_target_pairs={{0,128},{32,160},{64,192},{96,224},{128,0},{160,32},{192,64},{224,... | collective-permute-start | bytes 405512 | tf_op jit(solution)/shard_map/ppermute | solution.py:491
  47.2 9.2 %collective-permute-start.10 = (f32[264,128]{1,0:T(8,128)S(1)}, f32[264,128]{1,0:T(8,128)S(1)}, u32[]{:S(2)}, u32[]{:S(2)}) collective-permute-start(f32[264,128]{1,0:T(8,128)S(1)} %shard_map.48.q0), channel_id=1, source_target_pairs={{0,64},{32,96},{64,128},{96,160},{128,192},{160,224},{192,0},{224,... | collective-permute-start | bytes 405512 | tf_op jit(solution)/shard_map/ppermute | solution.py:491
  62.6 13.6 %collective-permute-start.16 = (f32[768,256]{1,0:T(8,128)S(1)}, f32[768,256]{1,0:T(8,128)S(1)}, u32[]{:S(2)}, u32[]{:S(2)}) collective-permute-start(f32[768,256]{1,0:T(8,128)S(1)} %shard_map.51.top_ref.refs_2_), channel_id=1, source_target_pairs={{0,1},{1,2},{2,3},{3,4},{4,5},{5,6},{6,7},{7,8},{8,9},{9,10},{10,1... | collective-permute-start | bytes 2359304 | tf_op jit(solution)/shard_map/ppermute | solution.py:486
  68.4 7.8 %collective-permute-start.13 = (f32[72,256]{1,0:T(8,128)S(1)}, f32[72,256]{1,0:T(8,128)S(1)}, u32[]{:S(2)}, u32[]{:S(2)}) collective-permute-start(f32[72,256]{1,0:T(8,128)S(1)} %get-tuple-element.37), channel_id=1, source_target_pairs={{0,64},{32,96},{64,128},{96,160},{128,192},{160,224},{192,0},{224,... | collective-permute-start | bytes 221192 | tf_op jit(solution)/shard_map/ppermute | solution.py:491
  68.6 7.6 %collective-permute-start.14 = (f32[72,256]{1,0:T(8,128)S(1)}, f32[72,256]{1,0:T(8,128)S(1)}, u32[]{:S(2)}, u32[]{:S(2)}) collective-permute-start(f32[72,256]{1,0:T(8,128)S(1)} %get-tuple-element.38), channel_id=1, source_target_pairs={{0,128},{32,160},{64,192},{96,224},{128,0},{160,32},{192,64},{224,... | collective-permute-start | bytes 221192 | tf_op jit(solution)/shard_map/ppermute | solution.py:491
  70.5 5.7 %collective-permute-start.15 = (f32[72,256]{1,0:T(8,128)S(1)}, f32[72,256]{1,0:T(8,128)S(1)}, u32[]{:S(2)}, u32[]{:S(2)}) collective-permute-start(f32[72,256]{1,0:T(8,128)S(1)} %get-tuple-element.39), channel_id=1, source_target_pairs={{0,192},{32,224},{64,0},{96,32},{128,64},{160,96},{192,128},{224,1... | collective-permute-start | bytes 221192 | tf_op jit(solution)/shard_map/ppermute | solution.py:491
  76.3 6.2 %collective-permute-start.17 = (f32[72,256]{1,0:T(8,128)S(1)}, f32[72,256]{1,0:T(8,128)S(1)}, u32[]{:S(2)}, u32[]{:S(2)}) collective-permute-start(f32[72,256]{1,0:T(8,128)S(1)} %shard_map.55), channel_id=1, source_target_pairs={{0,32},{32,0},{64,96},{96,64},{128,160},{160,128},{192,224},{224,1... | collective-permute-start | bytes 221192 | tf_op jit(solution)/shard_map/ppermute | solution.py:497
  82.5 25.1 %collective-permute-start.23 = (f32[1280,256]{1,0:T(8,128)S(1)}, f32[1280,256]{1,0:T(8,128)S(1)}, u32[]{:S(2)}, u32[]{:S(2)}) collective-permute-start(f32[1280,256]{1,0:T(8,128)S(1)} %shard_map.59), channel_id=1, source_target_pairs={{0,1},{1,2},{2,3},{3,4},{4,5},{5,6},{6,7},{7,8},{8,9},{9,10},{10,1... | collective-permute-start | bytes 3932168 | tf_op jit(solution)/shard_map/ppermute | solution.py:486
  84.8 5.9 %collective-permute-start.19 = (f32[72,256]{1,0:T(8,128)S(1)}, f32[72,256]{1,0:T(8,128)S(1)}, u32[]{:S(2)}, u32[]{:S(2)}) collective-permute-start(f32[72,256]{1,0:T(8,128)S(1)} %add.4.q0.refs_1_), channel_id=1, source_target_pairs={{0,128},{32,160},{64,192},{96,224},{128,0},{160,32},{192,64},{224,... | collective-permute-start | bytes 221192 | tf_op jit(solution)/shard_map/ppermute | solution.py:491
  85.4 6.0 %collective-permute-start.18 = (f32[72,256]{1,0:T(8,128)S(1)}, f32[72,256]{1,0:T(8,128)S(1)}, u32[]{:S(2)}, u32[]{:S(2)}) collective-permute-start(f32[72,256]{1,0:T(8,128)S(1)} %add.4.q0.refs_1_), channel_id=1, source_target_pairs={{0,64},{32,96},{64,128},{96,160},{128,192},{160,224},{192,0},{224,... | collective-permute-start | bytes 221192 | tf_op jit(solution)/shard_map/ppermute | solution.py:491
  96.7 10.8 %collective-permute-start.24 = (f32[512,256]{1,0:T(8,128)S(1)}, f32[512,256]{1,0:T(8,128)S(1)}, u32[]{:S(2)}, u32[]{:S(2)}) collective-permute-start(f32[512,256]{1,0:T(8,128)S(1)} %get-tuple-element.41.refs_3_), channel_id=1, source_target_pairs={{0,1},{1,2},{2,3},{3,4},{4,5},{5,6},{6,7},{7,8},{8,9},{9,10},{10,1... | collective-permute-start | bytes 1572872 | tf_op jit(solution)/shard_map/ppermute | solution.py:486
  102.2 13.7 %collective-permute-start.21 = (f32[512,256]{1,0:T(8,128)S(1)}, f32[512,256]{1,0:T(8,128)S(1)}, u32[]{:S(2)}, u32[]{:S(2)}) collective-permute-start(f32[512,256]{1,0:T(8,128)S(1)} %get-tuple-element.43), channel_id=1, source_target_pairs={{0,1},{1,2},{2,3},{3,4},{4,5},{5,6},{6,7},{7,8},{8,9},{9,10},{10,1... | collective-permute-start | bytes 1572872 | tf_op jit(solution)/shard_map/ppermute | solution.py:486
  102.8 13.2 %collective-permute-start.22 = (f32[256,256]{1,0:T(8,128)S(1)}, f32[256,256]{1,0:T(8,128)S(1)}, u32[]{:S(2)}, u32[]{:S(2)}) collective-permute-start(f32[256,256]{1,0:T(8,128)S(1)} %get-tuple-element.44), channel_id=1, source_target_pairs={{0,1},{1,2},{2,3},{3,4},{4,5},{5,6},{6,7},{7,8},{8,9},{9,10},{10,1... | collective-permute-start | bytes 786440 | tf_op jit(solution)/shard_map/ppermute | solution.py:486
  (2 other events, 21.6 us)
where the time goes:
time: 117 us
  waiting for transfers between devices  44.6 us (38%)
  Pallas kernels  42.6 us (36%)
  starting transfers between devices  28.8 us (25%)
    ppermute x15, waiting for transfers between devices, along_y(): lax.ppermute(array, 'row', [(2 * y + h, 2 * ((y + by) % length) + h) for...  22 us
    ppermute x15, starting transfers between devices, along_y(): lax.ppermute(array, 'row', [(2 * y + h, 2 * ((y + by) % length) + h) for...  20.9 us
    pallas_call x6, Pallas kernels, rotated(): pl.pallas_call(functools.partial(apply_kernel, listed, copied, len(arrays...  15.5 us
    ppermute x8, waiting for transfers between devices, passed_along(): lax.ppermute(array, 'pair', [(i, (i + by) % length) for i in range(length)])  15.2 us
    pallas_call x2, Pallas kernels, rotation(): pl.pallas_call(rotation_kernel, out_shape=[half, half, jax.ShapeDtypeStru...  10.8 us
    ppermute x2, waiting for transfers between devices, across_x(): lax.ppermute(array, 'row', [(i, i ^ 1) for i in range(lax.axis_size('row'...  7.32 us
    ppermute x2, starting transfers between devices, across_x(): lax.ppermute(array, 'row', [(i, i ^ 1) for i in range(lax.axis_size('row'...  6.58 us
    pallas_call x1, Pallas kernels, second_rotation(): pl.pallas_call(second_rotation_kernel, out_shape=[half, half], in_specs=[...  5.3 us
  transfers between devices with their start and end apart: 25, of which 16 were waited for; matrix products, arithmetic and copies ran while one was open for 0% of the time, Pallas kernels for 32%

commit v1 on v0

--- a/solution.py
+++ b/solution.py
@@ -137,14 +137,23 @@
     for part in range(rows // size):
         for copy in copies(part):
             copy.start()
-    add_rows(accs, loaded_ref[:size], loaded_ref[size:], True)
+    for acc in accs:
+        acc[...] = jnp.zeros_like(acc)
+
+    @pl.loop(0, size // BLOCK)
+    def _(step):
+        start = pl.multiple_of(step * BLOCK, BLOCK)
+        add_rows(accs, loaded_ref[pl.ds(start, BLOCK)], loaded_ref[pl.ds(size + start, BLOCK)], False)
 
     @pl.loop(0, rows // size)
     def _(part):
         for copy in copies(part):
             copy.wait()
-        start = pl.multiple_of(part * size, size)
-        add_rows(accs, rest[pl.ds(start, size)], rest[pl.ds(pl.multiple_of(rows + start, size), size)], False)
+
+        @pl.loop(0, size // BLOCK)
+        def _(step):
+            start = pl.multiple_of(part * size + step * BLOCK, BLOCK)
+            add_rows(accs, rest[pl.ds(start, BLOCK)], rest[pl.ds(rows + start, BLOCK)], False)
 
     put_pieces(accs, pieces, outs, where_ref[0])
 
@@ -204,10 +213,10 @@
     cross[...] = cross_ref[...]
     squares[...] = squares_ref[...]
 
-    @pl.loop(0, top_ref.shape[0] // 512)
+    @pl.loop(0, top_ref.shape[0] // BLOCK)
     def _(step):
-        begin = pl.multiple_of(step * 512, 512)
-        add_cross(cross, squares, top_ref[pl.ds(begin, 512)], bottom_ref[pl.ds(early + begin, 512)], False)
+        begin = pl.multiple_of(step * BLOCK, BLOCK)
+        add_cross(cross, squares, top_ref[pl.ds(begin, BLOCK)], bottom_ref[pl.ds(early + begin, BLOCK)], False)
 
     for idx in range(4):
         pieces[idx, :Q] = cross[idx * Q:(idx + 1) * Q]
@@ -518,7 +527,7 @@
     total = summed([total, across_x(total)], [raw])
     total_prev = passed_along(total)
     first, second, whole = rotation(where, gathered_quarters(total))
-    (sent,) = rotated([(own_b, 0, own_b, late, late, first, [(0, 0)])], [(late, False)], after=[total_prev], rolled=(BLOCK, 0))
+    (sent,) = rotated([(own_b, 0, own_b, late, late, first, [(0, 0)])], [(late, False)], after=[total_prev], rolled=(512, 0))
     quarters_prev = gathered_quarters(tied(total_prev, [sent]))
     sent = passed_along(sent)
     (bottom,) = rotated(
@@ -564,7 +573,6 @@
             (ship, MORE, ship, mid, mid - MORE, first_prev, [(0, RAW + MORE)]),
         ],
         [(rows, True)],
-        rolled=(BLOCK, 0),
     )
     return (with_last(top_out, out_late), bottom_out)
 

time: 117 us -> 119 us (1.017)
    pallas_call x6, Pallas kernels: 15.5 us -> 14.2 us  [rotated(): pl.pallas_call(functools.partial(apply_kernel, listed, copied, len(arrays...]
    pallas_call x1, Pallas kernels: 4.34 us -> 5.62 us  [first_gram(): pl.pallas_call(first_gram_kernel, out_shape=[jax.ShapeDtypeStruct((PIECE,...]
  transfers between devices with their start and end apart: 25 -> 25, of which waited for: 16 -> 16; matrix products, arithmetic and copies ran while one was open for 0% -> 0% of each run, Pallas kernels for 32% -> 33%
where the time goes in v1:
time: 119 us; the launch traced here: 118 us
  waiting for transfers between devices  45.5 us (38%)
  Pallas kernels  43.1 us (36%)
  starting transfers between devices  28.5 us (24%)
    ppermute x15, waiting for transfers between devices, along_y(): lax.ppermute(array, 'row', [(2 * y + h, 2 * ((y + by) % length) + h) for...  22.7 us
    ppermute x15, starting transfers between devices, along_y(): lax.ppermute(array, 'row', [(2 * y + h, 2 * ((y + by) % length) + h) for...  20.6 us
    ppermute x8, waiting for transfers between devices, passed_along(): lax.ppermute(array, 'pair', [(i, (i + by) % length) for i in range(length)])  15.8 us
    pallas_call x6, Pallas kernels, rotated(): pl.pallas_call(functools.partial(apply_kernel, listed, copied, len(arrays...  14.2 us
    pallas_call x2, Pallas kernels, rotation(): pl.pallas_call(rotation_kernel, out_shape=[half, half, jax.ShapeDtypeStru...  10.8 us
    ppermute x2, waiting for transfers between devices, across_x(): lax.ppermute(array, 'row', [(i, i ^ 1) for i in range(lax.axis_size('row'...  7.02 us
    ppermute x2, starting transfers between devices, across_x(): lax.ppermute(array, 'row', [(i, i ^ 1) for i in range(lax.axis_size('row'...  6.58 us
    pallas_call x1, Pallas kernels, first_gram(): pl.pallas_call(first_gram_kernel, out_shape=[jax.ShapeDtypeStruct((PIECE,...  5.62 us
  transfers between devices with their start and end apart: 25, of which 16 were waited for; matrix products, arithmetic and copies ran while one was open for 0% of the time, Pallas kernels for 33%

profile of v1, /device:TPU:128, one launch (start us, length us, event | category | flops | bytes accessed | tf_op | source)
XLA Modules:
  0.0 118.3 jit_solution(1110675965507317116)
XLA Ops:
  2.0 5.6 %shard_map.42 = (f32[264,128]{1,0:T(8,128)S(1)}, f32[264,128]{1,0:T(8,128)S(1)}, f32[264,128]{1,0:T(8,128)S(1)}, f32[264,128]{1,0:T(8,128)S(1)}, f32[3072,256]{1,0:T(8,128)}) custom-call(s32[1]{0:T(128)} %bitcast.where_ref, f32[1024,256]{1,0:T(8,128)S(1)} %shard_map.41.loaded_ref.refs_0_, f32[2048,256]{1,0:T(8,128)} %top_ref.3, f32[2048,256]{1,0:T(8,128)} %bottom_ref.3), custom_call_target="tpu_custom_call" | custom-call | flops 1879048192 | bytes 4194304 | tf_op jit(solution)/shard_map/pallas_call | solution.py:163
  9.2 2.9 %collective-permute-start.1 = (f32[264,128]{1,0:T(8,128)S(1)}, f32[264,128]{1,0:T(8,128)S(1)}, u32[]{:S(2)}, u32[]{:S(2)}) collective-permute-start(f32[264,128]{1,0:T(8,128)S(1)} %get-tuple-element.28), channel_id=1, source_target_pairs={{0,128},{32,160},{64,192},{96,224},{128,0},{160,32},{192,64},{224,... | collective-permute-start | bytes 405512 | tf_op jit(solution)/shard_map/ppermute | solution.py:500
  14.7 4.2 %collective-permute-done.1.refs_2_ = f32[264,128]{1,0:T(8,128)S(1)} collective-permute-done((f32[264,128]{1,0:T(8,128)S(1)}, f32[264,128]{1,0:T(8,128)S(1)}, u32[]{:S(2)}, u32[]{:S(2)}) %collective-permute-start.1) | collective-permute-done | bytes 135200 | tf_op jit(solution)/shard_map/ppermute | solution.py:500
  19.0 3.3 %collective-permute-start.3 = (f32[264,128]{1,0:T(8,128)S(1)}, f32[264,128]{1,0:T(8,128)S(1)}, u32[]{:S(2)}, u32[]{:S(2)}) collective-permute-start(f32[264,128]{1,0:T(8,128)S(1)} %shard_map.43.refs_0_), channel_id=1, source_target_pairs={{0,32},{32,0},{64,96},{96,64},{128,160},{160,128},{192,224},{224,1... | collective-permute-start | bytes 405512 | tf_op jit(solution)/shard_map/ppermute | solution.py:506
  22.3 4.1 %collective-permute-done.3.refs_1_ = f32[264,128]{1,0:T(8,128)S(1)} collective-permute-done((f32[264,128]{1,0:T(8,128)S(1)}, f32[264,128]{1,0:T(8,128)S(1)}, u32[]{:S(2)}, u32[]{:S(2)}) %collective-permute-start.3) | collective-permute-done | bytes 135200 | tf_op jit(solution)/shard_map/ppermute | solution.py:506
  26.5 2.7 %collective-permute-start.7 = (f32[264,128]{1,0:T(8,128)S(1)}, f32[264,128]{1,0:T(8,128)S(1)}, u32[]{:S(2)}, u32[]{:S(2)}) collective-permute-start(f32[264,128]{1,0:T(8,128)S(1)} %shard_map.44.q0), channel_id=1, source_target_pairs={{0,192},{32,224},{64,0},{96,32},{128,64},{160,96},{192,128},{224,1... | collective-permute-start | bytes 405512 | tf_op jit(solution)/shard_map/ppermute | solution.py:500
  30.8 3.5 %collective-permute-done.7.q3 = f32[264,128]{1,0:T(8,128)S(1)} collective-permute-done((f32[264,128]{1,0:T(8,128)S(1)}, f32[264,128]{1,0:T(8,128)S(1)}, u32[]{:S(2)}, u32[]{:S(2)}) %collective-permute-start.7) | collective-permute-done | bytes 135200 | tf_op jit(solution)/shard_map/ppermute | solution.py:500
  34.3 2.3 %collective-permute-done.6.q2 = f32[264,128]{1,0:T(8,128)S(1)} collective-permute-done((f32[264,128]{1,0:T(8,128)S(1)}, f32[264,128]{1,0:T(8,128)S(1)}, u32[]{:S(2)}, u32[]{:S(2)}) %collective-permute-start.6) | collective-permute-done | bytes 135200 | tf_op jit(solution)/shard_map/ppermute | solution.py:500
  38.0 5.4 %shard_map.45 = (f32[512,256]{1,0:T(8,128)S(1)}, f32[512,256]{1,0:T(8,128)S(1)}, f32[512,512]{1,0:T(8,128)S(1)}) custom-call(s32[1]{0:T(128)} %bitcast.where_ref, f32[264,128]{1,0:T(8,128)S(1)} %shard_map.44.q0, f32[264,128]{1,0:T(8,128)S(1)} %collective-permute-done.5.q1, f32[264,128]{1,0:T(8,128)S(1)} %collective-permute-done.6.q2, ...), custom_call_target="tpu_custom_call" | custom-call | flops 3758096384 | bytes 2097152 | tf_op jit(solution)/shard_map/pallas_call | solution.py:324
  49.6 3.1 %shard_map.47.refs_1_.bottom_ref = f32[2048,256]{1,0:T(8,128)S(1)} custom-call(f32[1024,256]{1,0:T(8,128)S(1)} %shard_map.41.loaded_ref.refs_0_, f32[3072,256]{1,0:T(8,128)S(1)} %copy-done, f32[512,256]{1,0:T(8,128)S(1)} %get-tuple-element.31.refs_2_.refs_0_), custom_call_target="tpu_custom_call" | custom-call | flops 1610612736 | bytes 6291456 | tf_op jit(solution)/shard_map/pallas_call | solution.py:428
  54.1 3.0 %collective-permute-done.10.q1 = f32[264,128]{1,0:T(8,128)S(1)} collective-permute-done((f32[264,128]{1,0:T(8,128)S(1)}, f32[264,128]{1,0:T(8,128)S(1)}, u32[]{:S(2)}, u32[]{:S(2)}) %collective-permute-start.10) | collective-permute-done | bytes 135200 | tf_op jit(solution)/shard_map/ppermute | solution.py:500
  57.1 5.4 %shard_map.50 = (f32[512,256]{1,0:T(8,128)S(1)}, f32[512,256]{1,0:T(8,128)S(1)}, f32[512,512]{1,0:T(8,128)S(1)}) custom-call(s32[1]{0:T(128)} %bitcast.where_ref, f32[264,128]{1,0:T(8,128)S(1)} %shard_map.48.q0, f32[264,128]{1,0:T(8,128)S(1)} %collective-permute-done.10.q1, f32[264,128]{1,0:T(8,128)S(1)} %collective-permute-done.11.q2, ...), custom_call_target="tpu_custom_call" | custom-call | flops 3758096384 | bytes 2097152 | tf_op jit(solution)/shard_map/pallas_call | solution.py:324
  64.0 3.5 %collective-permute-done.9.top_ref.refs_0_ = f32[1536,256]{1,0:T(8,128)S(1)} collective-permute-done((f32[1536,256]{1,0:T(8,128)S(1)}, f32[1536,256]{1,0:T(8,128)S(1)}, u32[]{:S(2)}, u32[]{:S(2)}) %collective-permute-start.9) | collective-permute-done | bytes 1572896 | tf_op jit(solution)/shard_map/ppermute | solution.py:495
  67.5 2.1 %shard_map.53 = (f32[72,256]{1,0:T(8,128)S(1)}, f32[72,256]{1,0:T(8,128)S(1)}, f32[72,256]{1,0:T(8,128)S(1)}, f32[72,256]{1,0:T(8,128)S(1)}, f32[1280,256]{1,0:T(8,128)S(1)}) custom-call(s32[1]{0:T(128)} %bitcast.where_ref, f32[1536,256]{1,0:T(8,128)S(1)} %collective-permute-done.9.top_ref.refs_0_, f32[2048,256]{1,0:T(8,128)S(1)} %shard_map.47.refs_1_.bottom_ref, ...), custom_call_target="tpu_custom_call" | custom-call | flops 402653184 | bytes 2097152 | tf_op jit(solution)/shard_map/pallas_call | solution.py:231
  74.8 2.1 %collective-permute-done.16.refs_4_.refs_0_ = f32[768,256]{1,0:T(8,128)S(1)} collective-permute-done((f32[768,256]{1,0:T(8,128)S(1)}, f32[768,256]{1,0:T(8,128)S(1)}, u32[]{:S(2)}, u32[]{:S(2)}) %collective-permute-start.16) | collective-permute-done | bytes 786464 | tf_op jit(solution)/shard_map/ppermute | solution.py:495
  77.0 3.3 %collective-permute-start.17 = (f32[72,256]{1,0:T(8,128)S(1)}, f32[72,256]{1,0:T(8,128)S(1)}, u32[]{:S(2)}, u32[]{:S(2)}) collective-permute-start(f32[72,256]{1,0:T(8,128)S(1)} %shard_map.55), channel_id=1, source_target_pairs={{0,32},{32,0},{64,96},{96,64},{128,160},{160,128},{192,224},{224,1... | collective-permute-start | bytes 221192 | tf_op jit(solution)/shard_map/ppermute | solution.py:506
  80.3 2.9 %collective-permute-done.17 = f32[72,256]{1,0:T(8,128)S(1)} collective-permute-done((f32[72,256]{1,0:T(8,128)S(1)}, f32[72,256]{1,0:T(8,128)S(1)}, u32[]{:S(2)}, u32[]{:S(2)}) %collective-permute-start.17) | collective-permute-done | bytes 73760 | tf_op jit(solution)/shard_map/ppermute | solution.py:506
  83.3 2.7 %collective-permute-start.20 = (f32[72,256]{1,0:T(8,128)S(1)}, f32[72,256]{1,0:T(8,128)S(1)}, u32[]{:S(2)}, u32[]{:S(2)}) collective-permute-start(f32[72,256]{1,0:T(8,128)S(1)} %add.4.q0.refs_1_), channel_id=1, source_target_pairs={{0,192},{32,224},{64,0},{96,32},{128,64},{160,96},{192,128},{224,1... | collective-permute-start | bytes 221192 | tf_op jit(solution)/shard_map/ppermute | solution.py:500
  88.7 3.2 %collective-permute-done.19.q2 = f32[72,256]{1,0:T(8,128)S(1)} collective-permute-done((f32[72,256]{1,0:T(8,128)S(1)}, f32[72,256]{1,0:T(8,128)S(1)}, u32[]{:S(2)}, u32[]{:S(2)}) %collective-permute-start.19) | collective-permute-done | bytes 73760 | tf_op jit(solution)/shard_map/ppermute | solution.py:500
  92.7 5.3 %shard_map.56 = (f32[512,256]{1,0:T(8,128)S(1)}, f32[512,256]{1,0:T(8,128)S(1)}) custom-call(s32[1]{0:T(128)} %bitcast.where_ref, f32[72,256]{1,0:T(8,128)S(1)} %add.4.q0.refs_1_, f32[72,256]{1,0:T(8,128)S(1)} %collective-permute-done.18.q1, f32[72,256]{1,0:T(8,128)S(1)} %collective-permute-done.19.q2, f32[72,256]{1,0:T(8,128)S(1)} %collective-permute-done.20.q3, ...), custom_call_target="tpu_custom_call" | custom-call | flops 3758096384 | bytes 2097152 | tf_op jit(solution)/shard_map/pallas_call | solution.py:358
  98.1 5.4 %shard_map.57 = (f32[512,256]{1,0:T(8,128)S(1)}, f32[256,256]{1,0:T(8,128)S(1)}, f32[2048,256]{1,0:T(8,128)}) custom-call(f32[1536,256]{1,0:T(8,128)S(1)} %collective-permute-done.9.top_ref.refs_0_, f32[2048,256]{1,0:T(8,128)S(1)} %shard_map.47.refs_1_.bottom_ref, f32[768,256]{1,0:T(8,128)S(1)} %shard_map.51.top_ref.refs_2_, ...), custom_call_target="tpu_custom_call" | custom-call | flops 2214592512 | bytes 8650752 | tf_op jit(solution)/shard_map/pallas_call | solution.py:428
  105.0 3.8 %collective-permute-done.24.refs_3_ = f32[512,256]{1,0:T(8,128)S(1)} collective-permute-done((f32[512,256]{1,0:T(8,128)S(1)}, f32[512,256]{1,0:T(8,128)S(1)}, u32[]{:S(2)}, u32[]{:S(2)}) %collective-permute-start.24) | collective-permute-done | bytes 524320 | tf_op jit(solution)/shard_map/ppermute | solution.py:495
  108.8 2.1 %shard_map.60.refs_2_ = f32[2048,256]{1,0:T(8,128)} custom-call(f32[768,256]{1,0:T(8,128)S(1)} %collective-permute-done.16.refs_4_.refs_0_, f32[512,256]{1,0:T(8,128)S(1)} %shard_map.58.refs_1_, f32[1280,256]{1,0:T(8,128)S(1)} %collective-permute-done.23.refs_2_, f32[512,256]{1,0:T(8,128)S(1)} %collective-permute-done.24.refs_3_), custom_call_target="tpu_custom_call" | custom-call | flops 1006632960 | bytes 3932160 | tf_op jit(solution)/shard_map/pallas_call | solution.py:428
  110.9 6.3 %collective-permute-done.22.refs_1_ = f32[256,256]{1,0:T(8,128)S(1)} collective-permute-done((f32[256,256]{1,0:T(8,128)S(1)}, f32[256,256]{1,0:T(8,128)S(1)}, u32[]{:S(2)}, u32[]{:S(2)}) %collective-permute-start.22) | collective-permute-done | bytes 262176 | tf_op jit(solution)/shard_map/ppermute | solution.py:495
  (50 shorter events, 29.0 us)
Async XLA Ops:
  1.9 24.6 %collective-permute-start.4 = (f32[1024,256]{1,0:T(8,128)S(1)}, f32[1024,256]{1,0:T(8,128)S(1)}, u32[]{:S(2)}, u32[]{:S(2)}) collective-permute-start(f32[1024,256]{1,0:T(8,128)S(1)} %shard_map.41.loaded_ref.refs_0_), channel_id=1, source_target_pairs={{0,1},{1,2},{2,3},{3,4},{4,5},{5,6},{6,7},{7,8},{8,9},{9,10},{10,1... | collective-permute-start | bytes 3145736 | tf_op jit(solution)/shard_map/ppermute | solution.py:495
  7.6 7.1 %collective-permute-start = (f32[264,128]{1,0:T(8,128)S(1)}, f32[264,128]{1,0:T(8,128)S(1)}, u32[]{:S(2)}, u32[]{:S(2)}) collective-permute-start(f32[264,128]{1,0:T(8,128)S(1)} %get-tuple-element.27), channel_id=1, source_target_pairs={{0,64},{32,96},{64,128},{96,160},{128,192},{160,224},{192,0},{224,... | collective-permute-start | bytes 405512 | tf_op jit(solution)/shard_map/ppermute | solution.py:500
  9.2 9.7 %collective-permute-start.1 = (f32[264,128]{1,0:T(8,128)S(1)}, f32[264,128]{1,0:T(8,128)S(1)}, u32[]{:S(2)}, u32[]{:S(2)}) collective-permute-start(f32[264,128]{1,0:T(8,128)S(1)} %get-tuple-element.28), channel_id=1, source_target_pairs={{0,128},{32,160},{64,192},{96,224},{128,0},{160,32},{192,64},{224,... | collective-permute-start | bytes 405512 | tf_op jit(solution)/shard_map/ppermute | solution.py:500
  12.1 6.8 %collective-permute-start.2 = (f32[264,128]{1,0:T(8,128)S(1)}, f32[264,128]{1,0:T(8,128)S(1)}, u32[]{:S(2)}, u32[]{:S(2)}) collective-permute-start(f32[264,128]{1,0:T(8,128)S(1)} %get-tuple-element.29), channel_id=1, source_target_pairs={{0,192},{32,224},{64,0},{96,32},{128,64},{160,96},{192,128},{224,1... | collective-permute-start | bytes 405512 | tf_op jit(solution)/shard_map/ppermute | solution.py:500
  19.0 7.4 %collective-permute-start.3 = (f32[264,128]{1,0:T(8,128)S(1)}, f32[264,128]{1,0:T(8,128)S(1)}, u32[]{:S(2)}, u32[]{:S(2)}) collective-permute-start(f32[264,128]{1,0:T(8,128)S(1)} %shard_map.43.refs_0_), channel_id=1, source_target_pairs={{0,32},{32,0},{64,96},{96,64},{128,160},{160,128},{192,224},{224,1... | collective-permute-start | bytes 405512 | tf_op jit(solution)/shard_map/ppermute | solution.py:506
  26.5 7.9 %collective-permute-start.7 = (f32[264,128]{1,0:T(8,128)S(1)}, f32[264,128]{1,0:T(8,128)S(1)}, u32[]{:S(2)}, u32[]{:S(2)}) collective-permute-start(f32[264,128]{1,0:T(8,128)S(1)} %shard_map.44.q0), channel_id=1, source_target_pairs={{0,192},{32,224},{64,0},{96,32},{128,64},{160,96},{192,128},{224,1... | collective-permute-start | bytes 405512 | tf_op jit(solution)/shard_map/ppermute | solution.py:500
  29.1 7.5 %collective-permute-start.6 = (f32[264,128]{1,0:T(8,128)S(1)}, f32[264,128]{1,0:T(8,128)S(1)}, u32[]{:S(2)}, u32[]{:S(2)}) collective-permute-start(f32[264,128]{1,0:T(8,128)S(1)} %shard_map.44.q0), channel_id=1, source_target_pairs={{0,128},{32,160},{64,192},{96,224},{128,0},{160,32},{192,64},{224,... | collective-permute-start | bytes 405512 | tf_op jit(solution)/shard_map/ppermute | solution.py:500
  30.3 7.7 %collective-permute-start.5 = (f32[264,128]{1,0:T(8,128)S(1)}, f32[264,128]{1,0:T(8,128)S(1)}, u32[]{:S(2)}, u32[]{:S(2)}) collective-permute-start(f32[264,128]{1,0:T(8,128)S(1)} %shard_map.44.q0), channel_id=1, source_target_pairs={{0,64},{32,96},{64,128},{96,160},{128,192},{160,224},{192,0},{224,... | collective-permute-start | bytes 405512 | tf_op jit(solution)/shard_map/ppermute | solution.py:500
  30.8 12.6 %collective-permute-start.8 = (f32[264,128]{1,0:T(8,128)S(1)}, f32[264,128]{1,0:T(8,128)S(1)}, u32[]{:S(2)}, u32[]{:S(2)}) collective-permute-start(f32[264,128]{1,0:T(8,128)S(1)} %shard_map.44.q0), channel_id=1, source_target_pairs={{0,1},{1,2},{2,3},{3,4},{4,5},{5,6},{6,7},{7,8},{8,9},{9,10},{10,1... | collective-permute-start | bytes 405512 | tf_op jit(solution)/shard_map/ppermute | solution.py:495
  45.3 22.2 %collective-permute-start.9 = (f32[1536,256]{1,0:T(8,128)S(1)}, f32[1536,256]{1,0:T(8,128)S(1)}, u32[]{:S(2)}, u32[]{:S(2)}) collective-permute-start(f32[1536,256]{1,0:T(8,128)S(1)} %shard_map.46.refs_1_), channel_id=1, source_target_pairs={{0,1},{1,2},{2,3},{3,4},{4,5},{5,6},{6,7},{7,8},{8,9},{9,10},{10,1... | collective-permute-start | bytes 4718600 | tf_op jit(solution)/shard_map/ppermute | solution.py:495
  45.6 7.1 %collective-permute-start.12 = (f32[264,128]{1,0:T(8,128)S(1)}, f32[264,128]{1,0:T(8,128)S(1)}, u32[]{:S(2)}, u32[]{:S(2)}) collective-permute-start(f32[264,128]{1,0:T(8,128)S(1)} %shard_map.48.q0), channel_id=1, source_target_pairs={{0,192},{32,224},{64,0},{96,32},{128,64},{160,96},{192,128},{224,1... | collective-permute-start | bytes 405512 | tf_op jit(solution)/shard_map/ppermute | solution.py:500
  46.2 7.9 %collective-permute-start.11 = (f32[264,128]{1,0:T(8,128)S(1)}, f32[264,128]{1,0:T(8,128)S(1)}, u32[]{:S(2)}, u32[]{:S(2)}) collective-permute-start(f32[264,128]{1,0:T(8,128)S(1)} %shard_map.48.q0), channel_id=1, source_target_pairs={{0,128},{32,160},{64,192},{96,224},{128,0},{160,32},{192,64},{224,... | collective-permute-start | bytes 405512 | tf_op jit(solution)/shard_map/ppermute | solution.py:500
  47.5 9.6 %collective-permute-start.10 = (f32[264,128]{1,0:T(8,128)S(1)}, f32[264,128]{1,0:T(8,128)S(1)}, u32[]{:S(2)}, u32[]{:S(2)}) collective-permute-start(f32[264,128]{1,0:T(8,128)S(1)} %shard_map.48.q0), channel_id=1, source_target_pairs={{0,64},{32,96},{64,128},{96,160},{128,192},{160,224},{192,0},{224,... | collective-permute-start | bytes 405512 | tf_op jit(solution)/shard_map/ppermute | solution.py:500
  63.4 13.6 %collective-permute-start.16 = (f32[768,256]{1,0:T(8,128)S(1)}, f32[768,256]{1,0:T(8,128)S(1)}, u32[]{:S(2)}, u32[]{:S(2)}) collective-permute-start(f32[768,256]{1,0:T(8,128)S(1)} %shard_map.51.top_ref.refs_2_), channel_id=1, source_target_pairs={{0,1},{1,2},{2,3},{3,4},{4,5},{5,6},{6,7},{7,8},{8,9},{9,10},{10,1... | collective-permute-start | bytes 2359304 | tf_op jit(solution)/shard_map/ppermute | solution.py:495
  69.7 7.3 %collective-permute-start.13 = (f32[72,256]{1,0:T(8,128)S(1)}, f32[72,256]{1,0:T(8,128)S(1)}, u32[]{:S(2)}, u32[]{:S(2)}) collective-permute-start(f32[72,256]{1,0:T(8,128)S(1)} %get-tuple-element.37), channel_id=1, source_target_pairs={{0,64},{32,96},{64,128},{96,160},{128,192},{160,224},{192,0},{224,... | collective-permute-start | bytes 221192 | tf_op jit(solution)/shard_map/ppermute | solution.py:500
  69.8 7.2 %collective-permute-start.14 = (f32[72,256]{1,0:T(8,128)S(1)}, f32[72,256]{1,0:T(8,128)S(1)}, u32[]{:S(2)}, u32[]{:S(2)}) collective-permute-start(f32[72,256]{1,0:T(8,128)S(1)} %get-tuple-element.38), channel_id=1, source_target_pairs={{0,128},{32,160},{64,192},{96,224},{128,0},{160,32},{192,64},{224,... | collective-permute-start | bytes 221192 | tf_op jit(solution)/shard_map/ppermute | solution.py:500
  77.0 6.2 %collective-permute-start.17 = (f32[72,256]{1,0:T(8,128)S(1)}, f32[72,256]{1,0:T(8,128)S(1)}, u32[]{:S(2)}, u32[]{:S(2)}) collective-permute-start(f32[72,256]{1,0:T(8,128)S(1)} %shard_map.55), channel_id=1, source_target_pairs={{0,32},{32,0},{64,96},{96,64},{128,160},{160,128},{192,224},{224,1... | collective-permute-start | bytes 221192 | tf_op jit(solution)/shard_map/ppermute | solution.py:506
  83.2 25.6 %collective-permute-start.23 = (f32[1280,256]{1,0:T(8,128)S(1)}, f32[1280,256]{1,0:T(8,128)S(1)}, u32[]{:S(2)}, u32[]{:S(2)}) collective-permute-start(f32[1280,256]{1,0:T(8,128)S(1)} %shard_map.59), channel_id=1, source_target_pairs={{0,1},{1,2},{2,3},{3,4},{4,5},{5,6},{6,7},{7,8},{8,9},{9,10},{10,1... | collective-permute-start | bytes 3932168 | tf_op jit(solution)/shard_map/ppermute | solution.py:495
  83.3 5.4 %collective-permute-start.20 = (f32[72,256]{1,0:T(8,128)S(1)}, f32[72,256]{1,0:T(8,128)S(1)}, u32[]{:S(2)}, u32[]{:S(2)}) collective-permute-start(f32[72,256]{1,0:T(8,128)S(1)} %add.4.q0.refs_1_), channel_id=1, source_target_pairs={{0,192},{32,224},{64,0},{96,32},{128,64},{160,96},{192,128},{224,1... | collective-permute-start | bytes 221192 | tf_op jit(solution)/shard_map/ppermute | solution.py:500
  86.0 5.9 %collective-permute-start.19 = (f32[72,256]{1,0:T(8,128)S(1)}, f32[72,256]{1,0:T(8,128)S(1)}, u32[]{:S(2)}, u32[]{:S(2)}) collective-permute-start(f32[72,256]{1,0:T(8,128)S(1)} %add.4.q0.refs_1_), channel_id=1, source_target_pairs={{0,128},{32,160},{64,192},{96,224},{128,0},{160,32},{192,64},{224,... | collective-permute-start | bytes 221192 | tf_op jit(solution)/shard_map/ppermute | solution.py:500
  86.7 6.0 %collective-permute-start.18 = (f32[72,256]{1,0:T(8,128)S(1)}, f32[72,256]{1,0:T(8,128)S(1)}, u32[]{:S(2)}, u32[]{:S(2)}) collective-permute-start(f32[72,256]{1,0:T(8,128)S(1)} %add.4.q0.refs_1_), channel_id=1, source_target_pairs={{0,64},{32,96},{64,128},{96,160},{128,192},{160,224},{192,0},{224,... | collective-permute-start | bytes 221192 | tf_op jit(solution)/shard_map/ppermute | solution.py:500
  98.0 10.8 %collective-permute-start.24 = (f32[512,256]{1,0:T(8,128)S(1)}, f32[512,256]{1,0:T(8,128)S(1)}, u32[]{:S(2)}, u32[]{:S(2)}) collective-permute-start(f32[512,256]{1,0:T(8,128)S(1)} %get-tuple-element.41.refs_3_), channel_id=1, source_target_pairs={{0,1},{1,2},{2,3},{3,4},{4,5},{5,6},{6,7},{7,8},{8,9},{9,10},{10,1... | collective-permute-start | bytes 1572872 | tf_op jit(solution)/shard_map/ppermute | solution.py:495
  103.5 13.7 %collective-permute-start.21 = (f32[512,256]{1,0:T(8,128)S(1)}, f32[512,256]{1,0:T(8,128)S(1)}, u32[]{:S(2)}, u32[]{:S(2)}) collective-permute-start(f32[512,256]{1,0:T(8,128)S(1)} %get-tuple-element.43), channel_id=1, source_target_pairs={{0,1},{1,2},{2,3},{3,4},{4,5},{5,6},{6,7},{7,8},{8,9},{9,10},{10,1... | collective-permute-start | bytes 1572872 | tf_op jit(solution)/shard_map/ppermute | solution.py:495
  104.0 13.2 %collective-permute-start.22 = (f32[256,256]{1,0:T(8,128)S(1)}, f32[256,256]{1,0:T(8,128)S(1)}, u32[]{:S(2)}, u32[]{:S(2)}) collective-permute-start(f32[256,256]{1,0:T(8,128)S(1)} %get-tuple-element.44), channel_id=1, source_target_pairs={{0,1},{1,2},{2,3},{3,4},{4,5},{5,6},{6,7},{7,8},{8,9},{9,10},{10,1... | collective-permute-start | bytes 786440 | tf_op jit(solution)/shard_map/ppermute | solution.py:495
  (2 other events, 22.2 us)

commit v2 on v0

--- a/solution.py
+++ b/solution.py
@@ -518,7 +518,7 @@
     total = summed([total, across_x(total)], [raw])
     total_prev = passed_along(total)
     first, second, whole = rotation(where, gathered_quarters(total))
-    (sent,) = rotated([(own_b, 0, own_b, late, late, first, [(0, 0)])], [(late, False)], after=[total_prev], rolled=(BLOCK, 0))
+    (sent,) = rotated([(own_b, 0, own_b, late, late, first, [(0, 0)])], [(late, False)], after=[total_prev], rolled=(512, 0))
     quarters_prev = gathered_quarters(tied(total_prev, [sent]))
     sent = passed_along(sent)
     (bottom,) = rotated(

time: 117 us -> 116 us (level)
  transfers between devices with their start and end apart: 25 -> 25, of which waited for: 16 -> 16; matrix products, arithmetic and copies ran while one was open for 0% -> 0% of each run, Pallas kernels for 32% -> 33%
where the time goes in v2:
time: 116 us
  waiting for transfers between devices  44.5 us (38%)
  Pallas kernels  42.1 us (36%)
  starting transfers between devices  28.6 us (25%)
    ppermute x15, waiting for transfers between devices, along_y(): lax.ppermute(array, 'row', [(2 * y + h, 2 * ((y + by) % length) + h) for...  22 us
    ppermute x15, starting transfers between devices, along_y(): lax.ppermute(array, 'row', [(2 * y + h, 2 * ((y + by) % length) + h) for...  20.9 us
    ppermute x8, waiting for transfers between devices, passed_along(): lax.ppermute(array, 'pair', [(i, (i + by) % length) for i in range(length)])  15.2 us
    pallas_call x6, Pallas kernels, rotated(): pl.pallas_call(functools.partial(apply_kernel, listed, copied, len(arrays...  14.9 us
    pallas_call x2, Pallas kernels, rotation(): pl.pallas_call(rotation_kernel, out_shape=[half, half, jax.ShapeDtypeStru...  10.8 us
    ppermute x2, waiting for transfers between devices, across_x(): lax.ppermute(array, 'row', [(i, i ^ 1) for i in range(lax.axis_size('row'...  7.3 us
    ppermute x2, starting transfers between devices, across_x(): lax.ppermute(array, 'row', [(i, i ^ 1) for i in range(lax.axis_size('row'...  6.38 us
    pallas_call x1, Pallas kernels, second_rotation(): pl.pallas_call(second_rotation_kernel, out_shape=[half, half], in_specs=[...  5.3 us
  transfers between devices with their start and end apart: 25, of which 16 were waited for; matrix products, arithmetic and copies ran while one was open for 0% of the time, Pallas kernels for 33%

profile of v2, /device:TPU:128, one launch (start us, length us, event | category | flops | bytes accessed | tf_op | source)
XLA Modules:
  0.0 116.3 jit_solution(2378715998354650027)
XLA Ops:
  2.0 4.3 %shard_map.42 = (f32[264,128]{1,0:T(8,128)S(1)}, f32[264,128]{1,0:T(8,128)S(1)}, f32[264,128]{1,0:T(8,128)S(1)}, f32[264,128]{1,0:T(8,128)S(1)}, f32[3072,256]{1,0:T(8,128)}) custom-call(s32[1]{0:T(128)} %bitcast.where_ref, f32[1024,256]{1,0:T(8,128)S(1)} %shard_map.41.loaded_ref.refs_0_, f32[2048,256]{1,0:T(8,128)} %top_ref.3, f32[2048,256]{1,0:T(8,128)} %bottom_ref.3), custom_call_target="tpu_custom_call" | custom-call | flops 1879048192 | bytes 4194304 | tf_op jit(solution)/shard_map/pallas_call | solution.py:154
  8.0 2.9 %collective-permute-start.1 = (f32[264,128]{1,0:T(8,128)S(1)}, f32[264,128]{1,0:T(8,128)S(1)}, u32[]{:S(2)}, u32[]{:S(2)}) collective-permute-start(f32[264,128]{1,0:T(8,128)S(1)} %get-tuple-element.28), channel_id=1, source_target_pairs={{0,128},{32,160},{64,192},{96,224},{128,0},{160,32},{192,64},{224,... | collective-permute-start | bytes 405512 | tf_op jit(solution)/shard_map/ppermute | solution.py:491
  13.4 4.2 %collective-permute-done.1.refs_2_ = f32[264,128]{1,0:T(8,128)S(1)} collective-permute-done((f32[264,128]{1,0:T(8,128)S(1)}, f32[264,128]{1,0:T(8,128)S(1)}, u32[]{:S(2)}, u32[]{:S(2)}) %collective-permute-start.1) | collective-permute-done | bytes 135200 | tf_op jit(solution)/shard_map/ppermute | solution.py:491
  17.7 3.3 %collective-permute-start.3 = (f32[264,128]{1,0:T(8,128)S(1)}, f32[264,128]{1,0:T(8,128)S(1)}, u32[]{:S(2)}, u32[]{:S(2)}) collective-permute-start(f32[264,128]{1,0:T(8,128)S(1)} %shard_map.43.refs_0_), channel_id=1, source_target_pairs={{0,32},{32,0},{64,96},{96,64},{128,160},{160,128},{192,224},{224,1... | collective-permute-start | bytes 405512 | tf_op jit(solution)/shard_map/ppermute | solution.py:497
  21.0 4.4 %collective-permute-done.3.refs_1_ = f32[264,128]{1,0:T(8,128)S(1)} collective-permute-done((f32[264,128]{1,0:T(8,128)S(1)}, f32[264,128]{1,0:T(8,128)S(1)}, u32[]{:S(2)}, u32[]{:S(2)}) %collective-permute-start.3) | collective-permute-done | bytes 135200 | tf_op jit(solution)/shard_map/ppermute | solution.py:497
  25.5 2.4 %collective-permute-start.7 = (f32[264,128]{1,0:T(8,128)S(1)}, f32[264,128]{1,0:T(8,128)S(1)}, u32[]{:S(2)}, u32[]{:S(2)}) collective-permute-start(f32[264,128]{1,0:T(8,128)S(1)} %shard_map.44.q0), channel_id=1, source_target_pairs={{0,192},{32,224},{64,0},{96,32},{128,64},{160,96},{192,128},{224,1... | collective-permute-start | bytes 405512 | tf_op jit(solution)/shard_map/ppermute | solution.py:491
  29.8 3.4 %collective-permute-done.7.q3 = f32[264,128]{1,0:T(8,128)S(1)} collective-permute-done((f32[264,128]{1,0:T(8,128)S(1)}, f32[264,128]{1,0:T(8,128)S(1)}, u32[]{:S(2)}, u32[]{:S(2)}) %collective-permute-start.7) | collective-permute-done | bytes 135200 | tf_op jit(solution)/shard_map/ppermute | solution.py:491
  33.2 2.2 %collective-permute-done.6.q2 = f32[264,128]{1,0:T(8,128)S(1)} collective-permute-done((f32[264,128]{1,0:T(8,128)S(1)}, f32[264,128]{1,0:T(8,128)S(1)}, u32[]{:S(2)}, u32[]{:S(2)}) %collective-permute-start.6) | collective-permute-done | bytes 135200 | tf_op jit(solution)/shard_map/ppermute | solution.py:491
  36.7 5.4 %shard_map.45 = (f32[512,256]{1,0:T(8,128)S(1)}, f32[512,256]{1,0:T(8,128)S(1)}, f32[512,512]{1,0:T(8,128)S(1)}) custom-call(s32[1]{0:T(128)} %bitcast.where_ref, f32[264,128]{1,0:T(8,128)S(1)} %shard_map.44.q0, f32[264,128]{1,0:T(8,128)S(1)} %collective-permute-done.5.q1, f32[264,128]{1,0:T(8,128)S(1)} %collective-permute-done.6.q2, ...), custom_call_target="tpu_custom_call" | custom-call | flops 3758096384 | bytes 2097152 | tf_op jit(solution)/shard_map/pallas_call | solution.py:315
  48.7 3.1 %shard_map.47.refs_1_.bottom_ref = f32[2048,256]{1,0:T(8,128)S(1)} custom-call(f32[1024,256]{1,0:T(8,128)S(1)} %shard_map.41.loaded_ref.refs_0_, f32[3072,256]{1,0:T(8,128)S(1)} %copy-done, f32[512,256]{1,0:T(8,128)S(1)} %get-tuple-element.31.refs_2_.refs_0_), custom_call_target="tpu_custom_call" | custom-call | flops 1610612736 | bytes 6291456 | tf_op jit(solution)/shard_map/pallas_call | solution.py:419
  52.9 3.0 %collective-permute-done.10.q1 = f32[264,128]{1,0:T(8,128)S(1)} collective-permute-done((f32[264,128]{1,0:T(8,128)S(1)}, f32[264,128]{1,0:T(8,128)S(1)}, u32[]{:S(2)}, u32[]{:S(2)}) %collective-permute-start.10) | collective-permute-done | bytes 135200 | tf_op jit(solution)/shard_map/ppermute | solution.py:491
  55.8 5.4 %shard_map.50 = (f32[512,256]{1,0:T(8,128)S(1)}, f32[512,256]{1,0:T(8,128)S(1)}, f32[512,512]{1,0:T(8,128)S(1)}) custom-call(s32[1]{0:T(128)} %bitcast.where_ref, f32[264,128]{1,0:T(8,128)S(1)} %shard_map.48.q0, f32[264,128]{1,0:T(8,128)S(1)} %collective-permute-done.10.q1, f32[264,128]{1,0:T(8,128)S(1)} %collective-permute-done.11.q2, ...), custom_call_target="tpu_custom_call" | custom-call | flops 3758096384 | bytes 2097152 | tf_op jit(solution)/shard_map/pallas_call | solution.py:315
  62.7 3.6 %collective-permute-done.9.top_ref.refs_0_ = f32[1536,256]{1,0:T(8,128)S(1)} collective-permute-done((f32[1536,256]{1,0:T(8,128)S(1)}, f32[1536,256]{1,0:T(8,128)S(1)}, u32[]{:S(2)}, u32[]{:S(2)}) %collective-permute-start.9) | collective-permute-done | bytes 1572896 | tf_op jit(solution)/shard_map/ppermute | solution.py:486
  70.0 2.2 %collective-permute-start.15 = (f32[72,256]{1,0:T(8,128)S(1)}, f32[72,256]{1,0:T(8,128)S(1)}, u32[]{:S(2)}, u32[]{:S(2)}) collective-permute-start(f32[72,256]{1,0:T(8,128)S(1)} %get-tuple-element.39), channel_id=1, source_target_pairs={{0,192},{32,224},{64,0},{96,32},{128,64},{160,96},{192,128},{224,1... | collective-permute-start | bytes 221192 | tf_op jit(solution)/shard_map/ppermute | solution.py:491
  73.4 2.3 %collective-permute-done.16.refs_4_.refs_0_ = f32[768,256]{1,0:T(8,128)S(1)} collective-permute-done((f32[768,256]{1,0:T(8,128)S(1)}, f32[768,256]{1,0:T(8,128)S(1)}, u32[]{:S(2)}, u32[]{:S(2)}) %collective-permute-start.16) | collective-permute-done | bytes 786464 | tf_op jit(solution)/shard_map/ppermute | solution.py:486
  75.7 3.0 %collective-permute-start.17 = (f32[72,256]{1,0:T(8,128)S(1)}, f32[72,256]{1,0:T(8,128)S(1)}, u32[]{:S(2)}, u32[]{:S(2)}) collective-permute-start(f32[72,256]{1,0:T(8,128)S(1)} %shard_map.55), channel_id=1, source_target_pairs={{0,32},{32,0},{64,96},{96,64},{128,160},{160,128},{192,224},{224,1... | collective-permute-start | bytes 221192 | tf_op jit(solution)/shard_map/ppermute | solution.py:497
  78.8 2.9 %collective-permute-done.17 = f32[72,256]{1,0:T(8,128)S(1)} collective-permute-done((f32[72,256]{1,0:T(8,128)S(1)}, f32[72,256]{1,0:T(8,128)S(1)}, u32[]{:S(2)}, u32[]{:S(2)}) %collective-permute-start.17) | collective-permute-done | bytes 73760 | tf_op jit(solution)/shard_map/ppermute | solution.py:497
  81.8 2.2 %collective-permute-start.20 = (f32[72,256]{1,0:T(8,128)S(1)}, f32[72,256]{1,0:T(8,128)S(1)}, u32[]{:S(2)}, u32[]{:S(2)}) collective-permute-start(f32[72,256]{1,0:T(8,128)S(1)} %add.4.q0.refs_1_), channel_id=1, source_target_pairs={{0,192},{32,224},{64,0},{96,32},{128,64},{160,96},{192,128},{224,1... | collective-permute-start | bytes 221192 | tf_op jit(solution)/shard_map/ppermute | solution.py:491
  86.7 3.2 %collective-permute-done.19.q2 = f32[72,256]{1,0:T(8,128)S(1)} collective-permute-done((f32[72,256]{1,0:T(8,128)S(1)}, f32[72,256]{1,0:T(8,128)S(1)}, u32[]{:S(2)}, u32[]{:S(2)}) %collective-permute-start.19) | collective-permute-done | bytes 73760 | tf_op jit(solution)/shard_map/ppermute | solution.py:491
  90.6 5.3 %shard_map.56 = (f32[512,256]{1,0:T(8,128)S(1)}, f32[512,256]{1,0:T(8,128)S(1)}) custom-call(s32[1]{0:T(128)} %bitcast.where_ref, f32[72,256]{1,0:T(8,128)S(1)} %add.4.q0.refs_1_, f32[72,256]{1,0:T(8,128)S(1)} %collective-permute-done.18.q1, f32[72,256]{1,0:T(8,128)S(1)} %collective-permute-done.19.q2, f32[72,256]{1,0:T(8,128)S(1)} %collective-permute-done.20.q3, ...), custom_call_target="tpu_custom_call" | custom-call | flops 3758096384 | bytes 2097152 | tf_op jit(solution)/shard_map/pallas_call | solution.py:349
  96.1 5.4 %shard_map.57 = (f32[512,256]{1,0:T(8,128)S(1)}, f32[256,256]{1,0:T(8,128)S(1)}, f32[2048,256]{1,0:T(8,128)}) custom-call(f32[1536,256]{1,0:T(8,128)S(1)} %collective-permute-done.9.top_ref.refs_0_, f32[2048,256]{1,0:T(8,128)S(1)} %shard_map.47.refs_1_.bottom_ref, f32[768,256]{1,0:T(8,128)S(1)} %shard_map.51.top_ref.refs_2_, ...), custom_call_target="tpu_custom_call" | custom-call | flops 2214592512 | bytes 8650752 | tf_op jit(solution)/shard_map/pallas_call | solution.py:419
  102.9 3.8 %collective-permute-done.24.refs_3_ = f32[512,256]{1,0:T(8,128)S(1)} collective-permute-done((f32[512,256]{1,0:T(8,128)S(1)}, f32[512,256]{1,0:T(8,128)S(1)}, u32[]{:S(2)}, u32[]{:S(2)}) %collective-permute-start.24) | collective-permute-done | bytes 524320 | tf_op jit(solution)/shard_map/ppermute | solution.py:486
  106.8 2.9 %shard_map.60.refs_2_ = f32[2048,256]{1,0:T(8,128)} custom-call(f32[768,256]{1,0:T(8,128)S(1)} %collective-permute-done.16.refs_4_.refs_0_, f32[512,256]{1,0:T(8,128)S(1)} %shard_map.58.refs_1_, f32[1280,256]{1,0:T(8,128)S(1)} %collective-permute-done.23.refs_2_, f32[512,256]{1,0:T(8,128)S(1)} %collective-permute-done.24.refs_3_), custom_call_target="tpu_custom_call" | custom-call | flops 1006632960 | bytes 3932160 | tf_op jit(solution)/shard_map/pallas_call | solution.py:419
  109.6 5.5 %collective-permute-done.22.refs_1_ = f32[256,256]{1,0:T(8,128)S(1)} collective-permute-done((f32[256,256]{1,0:T(8,128)S(1)}, f32[256,256]{1,0:T(8,128)S(1)}, u32[]{:S(2)}, u32[]{:S(2)}) %collective-permute-start.22) | collective-permute-done | bytes 262176 | tf_op jit(solution)/shard_map/ppermute | solution.py:486
  (50 shorter events, 29.0 us)
Async XLA Ops:
  1.9 23.6 %collective-permute-start.4 = (f32[1024,256]{1,0:T(8,128)S(1)}, f32[1024,256]{1,0:T(8,128)S(1)}, u32[]{:S(2)}, u32[]{:S(2)}) collective-permute-start(f32[1024,256]{1,0:T(8,128)S(1)} %shard_map.41.loaded_ref.refs_0_), channel_id=1, source_target_pairs={{0,1},{1,2},{2,3},{3,4},{4,5},{5,6},{6,7},{7,8},{8,9},{9,10},{10,1... | collective-permute-start | bytes 3145736 | tf_op jit(solution)/shard_map/ppermute | solution.py:486
  6.3 7.1 %collective-permute-start = (f32[264,128]{1,0:T(8,128)S(1)}, f32[264,128]{1,0:T(8,128)S(1)}, u32[]{:S(2)}, u32[]{:S(2)}) collective-permute-start(f32[264,128]{1,0:T(8,128)S(1)} %get-tuple-element.27), channel_id=1, source_target_pairs={{0,64},{32,96},{64,128},{96,160},{128,192},{160,224},{192,0},{224,... | collective-permute-start | bytes 405512 | tf_op jit(solution)/shard_map/ppermute | solution.py:491
  8.0 9.7 %collective-permute-start.1 = (f32[264,128]{1,0:T(8,128)S(1)}, f32[264,128]{1,0:T(8,128)S(1)}, u32[]{:S(2)}, u32[]{:S(2)}) collective-permute-start(f32[264,128]{1,0:T(8,128)S(1)} %get-tuple-element.28), channel_id=1, source_target_pairs={{0,128},{32,160},{64,192},{96,224},{128,0},{160,32},{192,64},{224,... | collective-permute-start | bytes 405512 | tf_op jit(solution)/shard_map/ppermute | solution.py:491
  10.9 6.8 %collective-permute-start.2 = (f32[264,128]{1,0:T(8,128)S(1)}, f32[264,128]{1,0:T(8,128)S(1)}, u32[]{:S(2)}, u32[]{:S(2)}) collective-permute-start(f32[264,128]{1,0:T(8,128)S(1)} %get-tuple-element.29), channel_id=1, source_target_pairs={{0,192},{32,224},{64,0},{96,32},{128,64},{160,96},{192,128},{224,1... | collective-permute-start | bytes 405512 | tf_op jit(solution)/shard_map/ppermute | solution.py:491
  17.7 7.7 %collective-permute-start.3 = (f32[264,128]{1,0:T(8,128)S(1)}, f32[264,128]{1,0:T(8,128)S(1)}, u32[]{:S(2)}, u32[]{:S(2)}) collective-permute-start(f32[264,128]{1,0:T(8,128)S(1)} %shard_map.43.refs_0_), channel_id=1, source_target_pairs={{0,32},{32,0},{64,96},{96,64},{128,160},{160,128},{192,224},{224,1... | collective-permute-start | bytes 405512 | tf_op jit(solution)/shard_map/ppermute | solution.py:497
  25.5 7.7 %collective-permute-start.7 = (f32[264,128]{1,0:T(8,128)S(1)}, f32[264,128]{1,0:T(8,128)S(1)}, u32[]{:S(2)}, u32[]{:S(2)}) collective-permute-start(f32[264,128]{1,0:T(8,128)S(1)} %shard_map.44.q0), channel_id=1, source_target_pairs={{0,192},{32,224},{64,0},{96,32},{128,64},{160,96},{192,128},{224,1... | collective-permute-start | bytes 405512 | tf_op jit(solution)/shard_map/ppermute | solution.py:491
  27.8 7.5 %collective-permute-start.6 = (f32[264,128]{1,0:T(8,128)S(1)}, f32[264,128]{1,0:T(8,128)S(1)}, u32[]{:S(2)}, u32[]{:S(2)}) collective-permute-start(f32[264,128]{1,0:T(8,128)S(1)} %shard_map.44.q0), channel_id=1, source_target_pairs={{0,128},{32,160},{64,192},{96,224},{128,0},{160,32},{192,64},{224,... | collective-permute-start | bytes 405512 | tf_op jit(solution)/shard_map/ppermute | solution.py:491
  29.3 7.5 %collective-permute-start.5 = (f32[264,128]{1,0:T(8,128)S(1)}, f32[264,128]{1,0:T(8,128)S(1)}, u32[]{:S(2)}, u32[]{:S(2)}) collective-permute-start(f32[264,128]{1,0:T(8,128)S(1)} %shard_map.44.q0), channel_id=1, source_target_pairs={{0,64},{32,96},{64,128},{96,160},{128,192},{160,224},{192,0},{224,... | collective-permute-start | bytes 405512 | tf_op jit(solution)/shard_map/ppermute | solution.py:491
  29.8 12.3 %collective-permute-start.8 = (f32[264,128]{1,0:T(8,128)S(1)}, f32[264,128]{1,0:T(8,128)S(1)}, u32[]{:S(2)}, u32[]{:S(2)}) collective-permute-start(f32[264,128]{1,0:T(8,128)S(1)} %shard_map.44.q0), channel_id=1, source_target_pairs={{0,1},{1,2},{2,3},{3,4},{4,5},{5,6},{6,7},{7,8},{8,9},{9,10},{10,1... | collective-permute-start | bytes 405512 | tf_op jit(solution)/shard_map/ppermute | solution.py:486
  44.1 22.2 %collective-permute-start.9 = (f32[1536,256]{1,0:T(8,128)S(1)}, f32[1536,256]{1,0:T(8,128)S(1)}, u32[]{:S(2)}, u32[]{:S(2)}) collective-permute-start(f32[1536,256]{1,0:T(8,128)S(1)} %shard_map.46.refs_1_), channel_id=1, source_target_pairs={{0,1},{1,2},{2,3},{3,4},{4,5},{5,6},{6,7},{7,8},{8,9},{9,10},{10,1... | collective-permute-start | bytes 4718600 | tf_op jit(solution)/shard_map/ppermute | solution.py:486
  44.3 7.5 %collective-permute-start.12 = (f32[264,128]{1,0:T(8,128)S(1)}, f32[264,128]{1,0:T(8,128)S(1)}, u32[]{:S(2)}, u32[]{:S(2)}) collective-permute-start(f32[264,128]{1,0:T(8,128)S(1)} %shard_map.48.q0), channel_id=1, source_target_pairs={{0,192},{32,224},{64,0},{96,32},{128,64},{160,96},{192,128},{224,1... | collective-permute-start | bytes 405512 | tf_op jit(solution)/shard_map/ppermute | solution.py:491
  45.0 7.9 %collective-permute-start.11 = (f32[264,128]{1,0:T(8,128)S(1)}, f32[264,128]{1,0:T(8,128)S(1)}, u32[]{:S(2)}, u32[]{:S(2)}) collective-permute-start(f32[264,128]{1,0:T(8,128)S(1)} %shard_map.48.q0), channel_id=1, source_target_pairs={{0,128},{32,160},{64,192},{96,224},{128,0},{160,32},{192,64},{224,... | collective-permute-start | bytes 405512 | tf_op jit(solution)/shard_map/ppermute | solution.py:491
  46.6 9.2 %collective-permute-start.10 = (f32[264,128]{1,0:T(8,128)S(1)}, f32[264,128]{1,0:T(8,128)S(1)}, u32[]{:S(2)}, u32[]{:S(2)}) collective-permute-start(f32[264,128]{1,0:T(8,128)S(1)} %shard_map.48.q0), channel_id=1, source_target_pairs={{0,64},{32,96},{64,128},{96,160},{128,192},{160,224},{192,0},{224,... | collective-permute-start | bytes 405512 | tf_op jit(solution)/shard_map/ppermute | solution.py:491
  62.1 13.6 %collective-permute-start.16 = (f32[768,256]{1,0:T(8,128)S(1)}, f32[768,256]{1,0:T(8,128)S(1)}, u32[]{:S(2)}, u32[]{:S(2)}) collective-permute-start(f32[768,256]{1,0:T(8,128)S(1)} %shard_map.51.top_ref.refs_2_), channel_id=1, source_target_pairs={{0,1},{1,2},{2,3},{3,4},{4,5},{5,6},{6,7},{7,8},{8,9},{9,10},{10,1... | collective-permute-start | bytes 2359304 | tf_op jit(solution)/shard_map/ppermute | solution.py:486
  67.9 7.8 %collective-permute-start.13 = (f32[72,256]{1,0:T(8,128)S(1)}, f32[72,256]{1,0:T(8,128)S(1)}, u32[]{:S(2)}, u32[]{:S(2)}) collective-permute-start(f32[72,256]{1,0:T(8,128)S(1)} %get-tuple-element.37), channel_id=1, source_target_pairs={{0,64},{32,96},{64,128},{96,160},{128,192},{160,224},{192,0},{224,... | collective-permute-start | bytes 221192 | tf_op jit(solution)/shard_map/ppermute | solution.py:491
  68.1 7.6 %collective-permute-start.14 = (f32[72,256]{1,0:T(8,128)S(1)}, f32[72,256]{1,0:T(8,128)S(1)}, u32[]{:S(2)}, u32[]{:S(2)}) collective-permute-start(f32[72,256]{1,0:T(8,128)S(1)} %get-tuple-element.38), channel_id=1, source_target_pairs={{0,128},{32,160},{64,192},{96,224},{128,0},{160,32},{192,64},{224,... | collective-permute-start | bytes 221192 | tf_op jit(solution)/shard_map/ppermute | solution.py:491
  70.0 5.7 %collective-permute-start.15 = (f32[72,256]{1,0:T(8,128)S(1)}, f32[72,256]{1,0:T(8,128)S(1)}, u32[]{:S(2)}, u32[]{:S(2)}) collective-permute-start(f32[72,256]{1,0:T(8,128)S(1)} %get-tuple-element.39), channel_id=1, source_target_pairs={{0,192},{32,224},{64,0},{96,32},{128,64},{160,96},{192,128},{224,1... | collective-permute-start | bytes 221192 | tf_op jit(solution)/shard_map/ppermute | solution.py:491
  75.7 5.9 %collective-permute-start.17 = (f32[72,256]{1,0:T(8,128)S(1)}, f32[72,256]{1,0:T(8,128)S(1)}, u32[]{:S(2)}, u32[]{:S(2)}) collective-permute-start(f32[72,256]{1,0:T(8,128)S(1)} %shard_map.55), channel_id=1, source_target_pairs={{0,32},{32,0},{64,96},{96,64},{128,160},{160,128},{192,224},{224,1... | collective-permute-start | bytes 221192 | tf_op jit(solution)/shard_map/ppermute | solution.py:497
  81.7 25.1 %collective-permute-start.23 = (f32[1280,256]{1,0:T(8,128)S(1)}, f32[1280,256]{1,0:T(8,128)S(1)}, u32[]{:S(2)}, u32[]{:S(2)}) collective-permute-start(f32[1280,256]{1,0:T(8,128)S(1)} %shard_map.59), channel_id=1, source_target_pairs={{0,1},{1,2},{2,3},{3,4},{4,5},{5,6},{6,7},{7,8},{8,9},{9,10},{10,1... | collective-permute-start | bytes 3932168 | tf_op jit(solution)/shard_map/ppermute | solution.py:486
  84.0 5.9 %collective-permute-start.19 = (f32[72,256]{1,0:T(8,128)S(1)}, f32[72,256]{1,0:T(8,128)S(1)}, u32[]{:S(2)}, u32[]{:S(2)}) collective-permute-start(f32[72,256]{1,0:T(8,128)S(1)} %add.4.q0.refs_1_), channel_id=1, source_target_pairs={{0,128},{32,160},{64,192},{96,224},{128,0},{160,32},{192,64},{224,... | collective-permute-start | bytes 221192 | tf_op jit(solution)/shard_map/ppermute | solution.py:491
  84.6 6.0 %collective-permute-start.18 = (f32[72,256]{1,0:T(8,128)S(1)}, f32[72,256]{1,0:T(8,128)S(1)}, u32[]{:S(2)}, u32[]{:S(2)}) collective-permute-start(f32[72,256]{1,0:T(8,128)S(1)} %add.4.q0.refs_1_), channel_id=1, source_target_pairs={{0,64},{32,96},{64,128},{96,160},{128,192},{160,224},{192,0},{224,... | collective-permute-start | bytes 221192 | tf_op jit(solution)/shard_map/ppermute | solution.py:491
  96.0 10.8 %collective-permute-start.24 = (f32[512,256]{1,0:T(8,128)S(1)}, f32[512,256]{1,0:T(8,128)S(1)}, u32[]{:S(2)}, u32[]{:S(2)}) collective-permute-start(f32[512,256]{1,0:T(8,128)S(1)} %get-tuple-element.41.refs_3_), channel_id=1, source_target_pairs={{0,1},{1,2},{2,3},{3,4},{4,5},{5,6},{6,7},{7,8},{8,9},{9,10},{10,1... | collective-permute-start | bytes 1572872 | tf_op jit(solution)/shard_map/ppermute | solution.py:486
  101.4 13.8 %collective-permute-start.21 = (f32[512,256]{1,0:T(8,128)S(1)}, f32[512,256]{1,0:T(8,128)S(1)}, u32[]{:S(2)}, u32[]{:S(2)}) collective-permute-start(f32[512,256]{1,0:T(8,128)S(1)} %get-tuple-element.43), channel_id=1, source_target_pairs={{0,1},{1,2},{2,3},{3,4},{4,5},{5,6},{6,7},{7,8},{8,9},{9,10},{10,1... | collective-permute-start | bytes 1572872 | tf_op jit(solution)/shard_map/ppermute | solution.py:486
  102.0 13.2 %collective-permute-start.22 = (f32[256,256]{1,0:T(8,128)S(1)}, f32[256,256]{1,0:T(8,128)S(1)}, u32[]{:S(2)}, u32[]{:S(2)}) collective-permute-start(f32[256,256]{1,0:T(8,128)S(1)} %get-tuple-element.44), channel_id=1, source_target_pairs={{0,1},{1,2},{2,3},{3,4},{4,5},{5,6},{6,7},{7,8},{8,9},{9,10},{10,1... | collective-permute-start | bytes 786440 | tf_op jit(solution)/shard_map/ppermute | solution.py:486
  (2 other events, 21.6 us)
